TPU v7x, 256 devices: a whole 4x4x8 slice. The times are simulated.
256 devices in a mesh: tm: 16 (over x, y_lo, core), space: 16 (over y_hi, z).
Axes of the slice: x: 4, y: 4 (y_hi: 2, y_lo: 2; y = y_hi * 2 + y_lo), z: 8, core: 2. Of those that a mesh axis runs over, the one named last changes fastest.
Arguments:
- video: bfloat16 [16, 32, 160, 512], P('tm', 'space'), may hold values from -8 to 8
- gain_conv: float32 [512], replicated, may hold values from 0.25 to 1.75
- conv_weight: bfloat16 [3, 3, 512, 512], replicated, may hold values from -0.09375 to 0.09375
- gain_space: float32 [512], replicated, may hold values from 0.25 to 1.75
- query_weight: bfloat16 [512, 512], replicated, may hold values from -2 to 2
- key_weight: bfloat16 [512, 512], replicated, may hold values from -1 to 1
- value_weight: bfloat16 [512, 512], replicated, may hold values from -0.25 to 0.25
- out_weight: bfloat16 [512, 512], replicated, may hold values from -0.25 to 0.25
- gain_time: float32 [512], replicated, may hold values from 0.25 to 1.75
- time_query: bfloat16 [512, 512], replicated, may hold values from -2 to 2
- time_key: bfloat16 [512, 512], replicated, may hold values from -1 to 1
- time_value: bfloat16 [512, 512], replicated, may hold values from -0.25 to 0.25
- time_out: bfloat16 [512, 512], replicated, may hold values from -0.25 to 0.25
Outputs:
- decoded: bfloat16 [16, 32, 160, 512], P('tm', 'space')
All inputs are finite; a program needn't handle non-finite values.
Results may differ from a plain program's by a relative error of at most 0.028.
Values may be sent and summed in bfloat16 or wider, within the bound.
A program may use at most 128 MiB of HBM per device.

v0:
```python
import math

import jax
import jax.numpy as jnp
from jax import lax
from jax.sharding import PartitionSpec as P

epsilon = 1e-06


def padded_2(block, sides, width):
    for axis, dim in sides:
        count = lax.axis_size(axis)
        forward = [(i, i + 1) for i in range(count - 1)]
        backward = [(target, source) for source, target in forward]
        low = lax.ppermute(
            lax.slice_in_dim(block, block.shape[dim] - width, None, axis=dim), axis, forward
        )
        high = lax.ppermute(lax.slice_in_dim(block, 0, width, axis=dim), axis, backward)
        block = jnp.concatenate([low, block, high], axis=dim)
    return block


def channel_norm(inputs, gains):
    values = inputs.astype(jnp.float32)
    average = jnp.mean(values, axis=-1, keepdims=True)
    centered = values - average
    spread = jnp.mean(centered * centered, axis=-1, keepdims=True)
    return centered * lax.rsqrt(spread + epsilon) * gains


def project(inputs, weight):
    return jnp.dot(inputs, weight, preferred_element_type=jnp.float32).astype(jnp.bfloat16)


def attend_block(running, query, key_rows, value_rows, score_scale):
    highest, totals, summed = running
    scores = jnp.dot(query, key_rows.T, preferred_element_type=jnp.float32) * score_scale
    new_high = jnp.maximum(highest, jnp.max(scores, axis=1))
    expd = jnp.exp(scores - new_high[:, None])
    totals = jnp.sum(expd, axis=1)
    summed = jnp.dot(expd.astype(jnp.bfloat16), value_rows, preferred_element_type=jnp.float32)
    return (new_high, totals, summed)


def local(
    video,
    gain_conv,
    conv_weight,
    gain_space,
    query_weight,
    key_weight,
    value_weight,
    out_weight,
    gain_time,
    time_query,
    time_key,
    time_value,
    time_out,
):
    row_count = video.shape[1]
    col_count = video.shape[2]
    channels = video.shape[3]
    tokens = row_count * col_count
    score_scale = 1.0 / math.sqrt(channels)
    frame = video[0]
    activated = jax.nn.silu(channel_norm(frame, gain_conv)).astype(jnp.bfloat16)
    padded = padded_2(activated, (("space", 0),), 1)
    padded = jnp.pad(padded, ((0, 0), (1, 1), (0, 0)))
    convolved = jnp.zeros((tokens, channels), jnp.float32)
    for tap_row in range(3):
        for tap_col in range(3):
            window = padded[tap_row : tap_row + row_count, tap_col : tap_col + col_count].reshape(
                tokens, channels
            )
            convolved = convolved + jnp.dot(
                window, conv_weight[tap_row, tap_col], preferred_element_type=jnp.float32
            )
    after_conv = (frame.reshape(tokens, channels).astype(jnp.float32) + convolved).astype(
        jnp.bfloat16
    )
    normed = channel_norm(after_conv, gain_space).astype(jnp.bfloat16)
    query = project(normed, query_weight)
    start_state = (
        jnp.full((tokens,), -1e30, jnp.float32),
        jnp.zeros((tokens,), jnp.float32),
        jnp.zeros((tokens, channels), jnp.float32),
    )
    key_rows = project(normed, key_weight)
    value_rows = project(normed, value_weight)
    highest, totals, summed = attend_block(
        start_state,
        query,
        lax.all_gather(key_rows, "space", axis=0, tiled=True),
        lax.all_gather(value_rows, "space", axis=0, tiled=True),
        score_scale,
    )
    mixed = (summed / totals[:, None]).astype(jnp.bfloat16)
    after_space = (
        after_conv.astype(jnp.float32)
        + jnp.dot(mixed, out_weight, preferred_element_type=jnp.float32)
    ).astype(jnp.bfloat16)
    time_normed = channel_norm(after_space, gain_time).astype(jnp.bfloat16)
    time_q = project(time_normed, time_query)[None]
    time_k = project(time_normed, time_key)[None]
    time_v = project(time_normed, time_value)[None]
    time_q, time_k, time_v = (
        lax.all_to_all(time_q, "tm", split_axis=1, concat_axis=0, tiled=True),
        lax.all_to_all(time_k, "tm", split_axis=1, concat_axis=0, tiled=True),
        lax.all_to_all(time_v, "tm", split_axis=1, concat_axis=0, tiled=True),
    )
    frame_count = time_q.shape[0]
    scores = (
        jnp.einsum("fnc,gnc->nfg", time_q, time_k, preferred_element_type=jnp.float32) * score_scale
    )
    later = lax.broadcasted_iota(jnp.int32, (frame_count, frame_count), 0) >= lax.broadcasted_iota(
        jnp.int32, (frame_count, frame_count), 1
    )
    scores = jnp.where(later[None], scores, jnp.float32(-1e30))
    highest = jnp.max(scores, axis=2, keepdims=True)
    expd = jnp.exp(scores - highest)
    totals = jnp.sum(expd, axis=2)
    temporal = jnp.einsum(
        "nfg,gnc->fnc", expd.astype(jnp.bfloat16), time_v, preferred_element_type=jnp.float32
    )
    temporal = (temporal / jnp.transpose(totals)[:, :, None]).astype(jnp.bfloat16)
    returned = lax.all_to_all(temporal, "tm", split_axis=0, concat_axis=1, tiled=True)
    decoded = after_space.astype(jnp.float32) + jnp.dot(
        returned[0], time_out, preferred_element_type=jnp.float32
    )
    return decoded.astype(jnp.bfloat16).reshape(1, row_count, col_count, channels)


def solution(mesh):
    return jax.shard_map(
        local,
        mesh=mesh,
        in_specs=(
            P("tm", "space", None, None),
            P(),
            P(),
            P(),
            P(),
            P(),
            P(),
            P(),
            P(),
            P(),
            P(),
            P(),
            P(),
        ),
        out_specs=P("tm", "space", None, None),
        check_vma=False,
    )
```

profile of v0, /device:TPU:1, one launch (start us, length us, event | category | flops | bytes accessed | tf_op | source)
XLA Modules:
  0.0 318.3 jit_solution(5381322476391295759)
XLA Ops:
  6.5 1.3 convert_reduce_fusion
  7.8 1.5 multiply_reduce_fusion.2
  9.3 1.3 multiply_convert_fusion.3
  10.7 4.4 %collective-permute-start = (bf16[1,160,512]{2,1,0:T(8,128)(2,1)S(1)}, bf16[1,160,512]{2,1,0:T(8,128)(2,1)S(1)}, u32[]{:S(2)}, u32[]{:S(2)}) collective-permute-start(bf16[1,160,512]{2,1,0:T(8,128)(2,1)S(1)} %get-tuple-element.13), channel_id=1, source_target_pairs={{0,1},{1,2},{2,3},{3,4},{4,5},{5,6},{6,7},{7,8},{8,9},{9,10},{10,1... | collective-permute-start | bytes 491528 | tf_op jit(solution)/shard_map/ppermute | solution.py:16
  15.0 1.3 collective-permute-start.1
  16.3 1.3 multiply_convert_fusion.2
  17.6 0.3 collective-permute-done
  17.9 4.2 %collective-permute-done.1 = bf16[1,160,512]{2,1,0:T(8,128)(2,1)S(1)} collective-permute-done((bf16[1,160,512]{2,1,0:T(8,128)(2,1)S(1)}, bf16[1,160,512]{2,1,0:T(8,128)(2,1)S(1)}, u32[]{:S(2)}, u32[]{:S(2)}) %collective-permute-start.1) | collective-permute-done | bytes 163872 | tf_op jit(solution)/shard_map/ppermute | solution.py:19
  22.1 0.2 fusion.31
  22.2 0.2 fusion.60
  22.5 0.3 fusion.41
  22.8 0.3 fusion.32
  23.2 0.3 convolution_add_fusion.8
  23.6 0.3 convolution_add_fusion.7
  23.9 0.3 convolution_add_fusion.6
  24.3 0.3 convolution_add_fusion.5
  24.6 0.3 convolution_add_fusion.4
  25.0 0.3 convolution_add_fusion.3
  25.3 0.5 fusion.62
  25.8 0.2 multiply_reduce_fusion.1
  26.1 0.2 multiply_convert_fusion.1
  26.3 1.0 convolution_convert_fusion.4
  27.3 0.2 all-gather.5.cloned.1.call-start
  27.6 1.1 convolution_convert_fusion.3
  28.7 107.4 %all-gather.3.cloned.1.call-done = bf16[5120,512]{1,0:T(8,128)(2,1)} async-done(((bf16[320,512]{1,0:T(8,128)(2,1)}), bf16[5120,512]{1,0:T(8,128)(2,1)}) %all-gather.3.cloned.1.call-update) | async-done | bytes 5242896 | tf_op jit(solution)/shard_map/all_gather | solution.py:94
  136.0 7.3 %fusion.63 = (f32[320]{0:T(512)S(1)}, f32[320,5120]{1,0:T(8,128)}) fusion(bf16[5120,512]{1,0:T(8,128)(2,1)} %all-gather.3.cloned.1.call-done, bf16[320,512]{1,0:T(8,128)(2,1)S(1)} %multiply_convert_fusion.1, bf16[512,512]{1,0:T(8,128)(2,1)S(1)} %copy-done), kind=kOutput, calls=%fused_computation.96 | convolution fusion | flops 1848934144 | bytes 12649728 | tf_op jit(solution)/shard_map/dot_general | solution.py:38
  143.3 3.9 %fusion = f32[320]{0:T(512)S(1)} fusion(f32[320,5120]{1,0:T(8,128)} %get-tuple-element.18, f32[320]{0:T(512)S(1)} %broadcast_maximum_fusion), kind=kLoop, calls=%fused_computation.2 | loop fusion | flops 3276480 | bytes 6556160 | tf_op jit(solution)/shard_map/reduce_sum | solution.py:41
  147.3 95.6 %all-gather.5.cloned.1.call-done = bf16[5120,512]{1,0:T(8,128)(2,1)} async-done(((bf16[320,512]{1,0:T(8,128)(2,1)}), bf16[5120,512]{1,0:T(8,128)(2,1)}) %all-gather.5.cloned.1.call-update) | async-done | bytes 5242896 | tf_op jit(solution)/shard_map/all_gather | solution.py:95
  243.0 6.6 %fusion.64 = (f32[320]{0:T(512)S(1)}, f32[320,512]{1,0:T(8,128)S(1)}) fusion(f32[320,512]{1,0:T(8,128)S(1)} %get-tuple-element.16, bf16[512,512]{1,0:T(8,128)(2,1)S(1)} %copy-done.11, bf16[5120,512]{1,0:T(8,128)(2,1)} %all-gather.5.cloned.1.call-done, f32[320,5120]{1,0:T(8,128)} %get-tuple-element.18, f32[320]{0:T(512)S(1)} %broadcast_maximum_fusion, ...), kind=kOutput, calls=%fused_computation.97 | convolution fusion | flops 1849753344 | bytes 13635328 | tf_op jit(solution)/shard_map/dot_general | solution.py:101
  249.6 0.2 multiply_reduce_fusion
  249.9 0.2 multiply_convert_fusion
  250.0 0.3 fusion.22
  250.4 0.5 copy.49
  250.9 0.6 broadcast.118
  251.5 2.7 reduce.9
  254.2 0.9 reshape.131
  255.0 7.7 %all-to-all-start.1 = ((bf16[16,2,5120]{2,1,0:T(2,128)(2,1)}), bf16[16,2,5120]{2,1,0:T(2,128)(2,1)S(1)}, u32[]{:S(2)}, u32[]{:S(2)}) async-start(bf16[16,2,5120]{2,1,0:T(2,128)(2,1)} %reshape.131), calls=%async_computation.1 | async-start | bytes 655360 | tf_op jit(solution)/shard_map/all_to_all | solution.py:108
  262.7 0.3 fusion.23
  263.1 0.5 copy.48
  263.6 2.7 reduce.8
  266.2 0.9 reshape.129
  267.1 3.6 %all-to-all-done.1 = bf16[16,2,5120]{2,1,0:T(2,128)(2,1)S(1)} async-done(((bf16[16,2,5120]{2,1,0:T(2,128)(2,1)}), bf16[16,2,5120]{2,1,0:T(2,128)(2,1)S(1)}, u32[]{:S(2)}, u32[]{:S(2)}) %all-to-all-start.1) | async-done | bytes 327712 | tf_op jit(solution)/shard_map/all_to_all | solution.py:108
  270.7 3.8 %all-to-all-start.2 = ((bf16[16,2,5120]{2,1,0:T(2,128)(2,1)}), bf16[16,2,5120]{2,1,0:T(2,128)(2,1)S(1)}, u32[]{:S(2)}, u32[]{:S(2)}) async-start(bf16[16,2,5120]{2,1,0:T(2,128)(2,1)} %reshape.129), calls=%async_computation.2 | async-start | bytes 655360 | tf_op jit(solution)/shard_map/all_to_all | solution.py:109
  274.6 0.3 fusion.21
  274.9 0.5 copy.50
  275.4 2.7 reduce.7
  278.1 0.9 reshape.127
  279.0 0.3 reshape.132
  279.2 3.4 %all-to-all-done.2 = bf16[16,2,5120]{2,1,0:T(2,128)(2,1)S(1)} async-done(((bf16[16,2,5120]{2,1,0:T(2,128)(2,1)}), bf16[16,2,5120]{2,1,0:T(2,128)(2,1)S(1)}, u32[]{:S(2)}, u32[]{:S(2)}) %all-to-all-start.2) | async-done | bytes 327712 | tf_op jit(solution)/shard_map/all_to_all | solution.py:109
  282.6 3.9 %all-to-all-start = ((bf16[16,2,5120]{2,1,0:T(2,128)(2,1)}), bf16[16,2,5120]{2,1,0:T(2,128)(2,1)S(1)}, u32[]{:S(2)}, u32[]{:S(2)}) async-start(bf16[16,2,5120]{2,1,0:T(2,128)(2,1)} %reshape.127), calls=%async_computation | async-start | bytes 655360 | tf_op jit(solution)/shard_map/all_to_all | solution.py:110
  286.5 1.9 bitcast_reduce_fusion
  288.4 0.1 all_to_all.17
  288.5 0.3 reshape.130
  288.8 1.9 bitcast_reduce_fusion.1
  290.7 0.8 all_to_all.19
  291.5 3.1 all-to-all-done
  294.6 0.3 reshape.128
  294.9 1.9 bitcast_reduce_fusion.2
  296.8 1.3 fusion.67
  298.2 0.3 fusion.9
  298.5 0.2 copy.30
  298.7 11.6 %all_to_all.45 = bf16[16,20,512]{2,1,0:T(8,128)(2,1)S(1)} all-to-all(bf16[16,20,512]{2,1,0:T(8,128)(2,1)S(1)} %copy.30), channel_id=1, replica_groups=mesh['tm'=16,'space'=16] {'tm'}, dimensions={0} | all-to-all | bytes 655360 | tf_op jit(solution)/shard_map/all_to_all | solution.py:127
  310.3 0.1 squeeze.40
  310.4 1.1 fusion.14
  (39 shorter events, 0.4 us)
Async XLA Ops:
  6.5 129.5 %copy-start = (bf16[512,512]{1,0:T(8,128)(2,1)S(1)}, bf16[512,512]{1,0:T(8,128)(2,1)}, u32[]{:S(2)}) copy-start(bf16[512,512]{1,0:T(8,128)(2,1)} %param.17) | copy-start | bytes 1572868
  6.5 129.5 %all-gather.3.cloned.1.call-start = ((), (), s32[]{:S(2)}) async-start(), calls=%async_computation.4 | async-start | bytes 5570560 | tf_op jit(solution)/shard_map/all_gather | solution.py:94
  6.5 15.9 %copy-start.2 = (bf16[3,3,512,512]{3,2,1,0:T(8,128)(2,1)S(1)}, bf16[3,3,512,512]{3,2,1,0:T(8,128)(2,1)}, u32[]{:S(2)}) copy-start(bf16[3,3,512,512]{3,2,1,0:T(8,128)(2,1)} %param.15) | copy-start | bytes 14155780
  10.7 7.2 %collective-permute-start = (bf16[1,160,512]{2,1,0:T(8,128)(2,1)S(1)}, bf16[1,160,512]{2,1,0:T(8,128)(2,1)S(1)}, u32[]{:S(2)}, u32[]{:S(2)}) collective-permute-start(bf16[1,160,512]{2,1,0:T(8,128)(2,1)S(1)} %get-tuple-element.13), channel_id=1, source_target_pairs={{0,1},{1,2},{2,3},{3,4},{4,5},{5,6},{6,7},{7,8},{8,9},{9,10},{10,1... | collective-permute-start | bytes 491528 | tf_op jit(solution)/shard_map/ppermute | solution.py:16
  15.0 7.0 %collective-permute-start.1 = (bf16[1,160,512]{2,1,0:T(8,128)(2,1)S(1)}, bf16[1,160,512]{2,1,0:T(8,128)(2,1)S(1)}, u32[]{:S(2)}, u32[]{:S(2)}) collective-permute-start(bf16[1,160,512]{2,1,0:T(8,128)(2,1)S(1)} %get-tuple-element.14), channel_id=1, source_target_pairs={{1,0},{2,1},{3,2},{4,3},{5,4},{6,5},{7,6},{8,7},{9,8},{10,9},{11,1... | collective-permute-start | bytes 491528 | tf_op jit(solution)/shard_map/ppermute | solution.py:19
  23.9 1.4 copy-start.1
  24.3 1.8 copy-start.9
  24.6 1.6 copy-start.4
  25.0 2.6 copy-start.5
  27.3 215.6 %all-gather.5.cloned.1.call-start = ((), (), s32[]{:S(2)}) async-start(), calls=%async_computation.5 | async-start | bytes 5570560 | tf_op jit(solution)/shard_map/all_gather | solution.py:95
  143.3 99.6 %copy-start.11 = (bf16[512,512]{1,0:T(8,128)(2,1)S(1)}, bf16[512,512]{1,0:T(8,128)(2,1)}, u32[]{:S(2)}) copy-start(bf16[512,512]{1,0:T(8,128)(2,1)} %param.20) | copy-start | bytes 1572868
  147.3 102.6 %copy-start.10 = (f32[512]{0:T(512)S(1)}, f32[512]{0:T(512)}, u32[]{:S(2)}) copy-start(f32[512]{0:T(512)} %param.21) | copy-start | bytes 6148
  147.3 102.7 %copy-start.6 = (bf16[512,512]{1,0:T(8,128)(2,1)S(1)}, bf16[512,512]{1,0:T(8,128)(2,1)}, u32[]{:S(2)}) copy-start(bf16[512,512]{1,0:T(8,128)(2,1)} %param.22) | copy-start | bytes 1572868
  249.6 13.1 %copy-start.7 = (bf16[512,512]{1,0:T(8,128)(2,1)S(1)}, bf16[512,512]{1,0:T(8,128)(2,1)}, u32[]{:S(2)}) copy-start(bf16[512,512]{1,0:T(8,128)(2,1)} %param.23) | copy-start | bytes 1572868
  249.9 24.7 %copy-start.8 = (bf16[512,512]{1,0:T(8,128)(2,1)S(1)}, bf16[512,512]{1,0:T(8,128)(2,1)}, u32[]{:S(2)}) copy-start(bf16[512,512]{1,0:T(8,128)(2,1)} %param.24) | copy-start | bytes 1572868
  255.0 15.7 %all-to-all-start.1 = ((bf16[16,2,5120]{2,1,0:T(2,128)(2,1)}), bf16[16,2,5120]{2,1,0:T(2,128)(2,1)S(1)}, u32[]{:S(2)}, u32[]{:S(2)}) async-start(bf16[16,2,5120]{2,1,0:T(2,128)(2,1)} %reshape.131), calls=%async_computation.1 | async-start | bytes 655360 | tf_op jit(solution)/shard_map/all_to_all | solution.py:108
  270.7 11.9 %all-to-all-start.2 = ((bf16[16,2,5120]{2,1,0:T(2,128)(2,1)}), bf16[16,2,5120]{2,1,0:T(2,128)(2,1)S(1)}, u32[]{:S(2)}, u32[]{:S(2)}) async-start(bf16[16,2,5120]{2,1,0:T(2,128)(2,1)} %reshape.129), calls=%async_computation.2 | async-start | bytes 655360 | tf_op jit(solution)/shard_map/all_to_all | solution.py:109
  282.6 12.0 %all-to-all-start = ((bf16[16,2,5120]{2,1,0:T(2,128)(2,1)}), bf16[16,2,5120]{2,1,0:T(2,128)(2,1)S(1)}, u32[]{:S(2)}, u32[]{:S(2)}) async-start(bf16[16,2,5120]{2,1,0:T(2,128)(2,1)} %reshape.127), calls=%async_computation | async-start | bytes 655360 | tf_op jit(solution)/shard_map/all_to_all | solution.py:110
  290.7 19.7 %copy-start.3 = (bf16[512,512]{1,0:T(8,128)(2,1)S(1)}, bf16[512,512]{1,0:T(8,128)(2,1)}, u32[]{:S(2)}) copy-start(bf16[512,512]{1,0:T(8,128)(2,1)} %param.25) | copy-start | bytes 1572868
Sparse Core Ops, SparseCore 0:
  27.4 108.5 all-gather.2
  138.6 104.3 all-gather.4
where the time goes:
time: 319 us; the launch traced here: 318 us
  waiting for transfers between devices  218 us (68%)
  matrix products  22.8 us (7%)
  starting transfers between devices  21.3 us (7%)
  other arithmetic  18.4 us (6%)
  between operations  13.9 us (4%)
  local copies, waits for them, and re-layouts  12.7 us (4%)
  blocking collectives  11.6 us (4%)
    all_gather x1, waiting for transfers between devices, local(): lax.all_gather(key_rows, 'space', axis=0, tiled=True)  107 us
    all_gather x1, waiting for transfers between devices, local(): lax.all_gather(value_rows, 'space', axis=0, tiled=True)  95.6 us
    all_to_all x1, blocking collectives, local(): lax.all_to_all(temporal, 'tm', split_axis=0, concat_axis=1, tiled=True)  11.6 us
    unnamed x3, other arithmetic  7.96 us
    all_to_all x1, starting transfers between devices, local(): lax.all_to_all(time_q, 'tm', split_axis=1, concat_axis=0, tiled=True)  7.7 us
    dot_general x1, matrix products, attend_block(): jnp.dot(query, key_rows.T, preferred_element_type=jnp.float32) * score_scale  7.33 us
    dot_general x1, matrix products, local(): jnp.dot(mixed, out_weight, preferred_element_type=jnp.float32)  6.62 us
  transfers between devices with their start and end apart: 7, of which 7 were waited for; matrix products, arithmetic and copies ran while one was open for 8% of the time, Pallas kernels for 0%

commit v1 on v0

v1 whole, which is shorter than its diff:
```python
import math

import jax
import jax.numpy as jnp
from jax import lax
from jax.experimental import pallas as pl
from jax.experimental.pallas import tpu as pltpu
from jax.sharding import PartitionSpec as P

epsilon = 1e-06
MESH = pl.DeviceIdType.MESH
XS, YL, CORES, YH, ZS = 4, 2, 2, 2, 8
TM = XS * YL * CORES
FRAMES = 16
W = 160
D = 512
T = 2 * W
HALF = T // 2
PIECE = 16
PIECES = T // PIECE
SCALE = 1.0 / math.sqrt(D)
LOG2E = math.log2(math.e)
BF = jnp.bfloat16
F32 = jnp.float32

ORDER = [(0, 0, 0)]
for ring, dist in [(0, 1), (1, 0), (0, 2), (1, 1), (0, 3), (1, 2), (0, 4), (1, 3), (1, 4)]:
    ORDER += [(ring, dist, 0)] if dist in (0, 4) else [(ring, dist, 0), (ring, dist, 1)]


def channel_norm(values, gains):
    average = jnp.mean(values, axis=-1, keepdims=True)
    centered = values - average
    spread = jnp.mean(centered * centered, axis=-1, keepdims=True)
    return centered * lax.rsqrt(spread + epsilon) * gains


def dot(a, b):
    return jnp.dot(a, b, preferred_element_type=F32)


def dot_t(a, b):
    return lax.dot_general(a, b, (((1,), (1,)), ((), ())), preferred_element_type=F32)


def second_owner(i):
    return i * 4 + (i % 2) * 2


def pick(t, values):
    out = jnp.int32(values[0])
    for k, v in enumerate(values):
        if k:
            out = jnp.where(t == k, jnp.int32(v), out)
    return out


def kernel(
    video, gain_conv, conv_w, gain_space, wq, wk, wv, wo, gain_time, tq, tk, tv, to,
    out,
    vid, halo, gc, gs, gt, cw, wq_v, wk_v, wv_v, wo_v, tq_v, tk_v, tv_v, to_v,
    act3, conv_acc, ac_mine, ac_t, nall, q_v, m_v, l_v, acc_v, as_t, tbuf, dbuf,
    load_sem, halo_send, halo_recv, swap_send, swap_recv,
    ring_send, sib_send, recv,
    a_send, a_recv, a_self, d_send, d_recv, d_self,
):
    tm = lax.axis_index("tm")
    sp = lax.axis_index("space")
    c = lax.rem(tm, 2)
    col = tm // 2
    h = sp // ZS
    z = lax.rem(sp, ZS)
    zp = lax.rem(z + 1, ZS)
    zm = lax.rem(z + ZS - 1, ZS)
    sibling = (col * 2 + 1 - c, sp)
    z_ids = ((tm, h * ZS + zp), (tm, h * ZS + zm))
    stays = c == h

    loads = []
    for i, (src, dst) in enumerate(
        [
            (video, vid), (gain_conv, gc), (conv_w.at[1], cw.at[1]), (conv_w.at[0], cw.at[0]),
            (conv_w.at[2], cw.at[2]), (gain_space, gs), (wq, wq_v), (wk, wk_v), (wv, wv_v), (wo, wo_v),
            (gain_time, gt), (tq, tq_v), (tk, tk_v), (tv, tv_v), (to, to_v),
        ]
    ):
        loads.append(pltpu.make_async_copy(src, dst, load_sem.at[i]))
        loads[-1].start()

    barrier = pltpu.get_barrier_semaphore()

    def greet(i, carry):
        other_tm = i // 2
        other_sp = lax.rem(i, 2) * ZS + z

        @pl.when(jnp.logical_or(other_tm != tm, other_sp != sp))
        def _():
            pl.semaphore_signal(barrier, inc=1, device_id=(other_tm, other_sp), device_id_type=MESH)

        return carry

    lax.fori_loop(0, TM * YH, greet, 0)
    for target in z_ids:
        pl.semaphore_signal(barrier, inc=1, device_id=target, device_id_type=MESH)
    crosses_down = sp == ZS - 1
    crosses_up = sp == ZS

    @pl.when(crosses_down)
    def _():
        pl.semaphore_signal(barrier, inc=1, device_id=(tm, ZS), device_id_type=MESH)

    @pl.when(crosses_up)
    def _():
        pl.semaphore_signal(barrier, inc=1, device_id=(tm, ZS - 1), device_id_type=MESH)

    crosses = jnp.where(jnp.logical_or(crosses_down, crosses_up), 1, 0)
    pl.semaphore_wait(barrier, TM * YH - 1 + 2 + crosses)

    has_up = sp > 0
    has_down = sp < YH * ZS - 1
    to_down = pltpu.make_async_remote_copy(
        src_ref=video.at[pl.ds(W, W)], dst_ref=halo.at[0], send_sem=halo_send.at[0], recv_sem=halo_recv.at[0],
        device_id=(tm, jnp.minimum(sp + 1, YH * ZS - 1)), device_id_type=MESH,
    )
    to_up = pltpu.make_async_remote_copy(
        src_ref=video.at[pl.ds(0, W)], dst_ref=halo.at[1], send_sem=halo_send.at[1], recv_sem=halo_recv.at[1],
        device_id=(tm, jnp.maximum(sp - 1, 0)), device_id_type=MESH,
    )

    @pl.when(has_down)
    def _():
        to_down.start()

    @pl.when(has_up)
    def _():
        to_up.start()

    loads[0].wait()
    loads[1].wait()
    col_index = lax.broadcasted_iota(jnp.int32, (W, D), 0)

    def activate(row, raw):
        u = channel_norm(raw.astype(F32), gc[...])
        u = (u / (1.0 + jnp.exp(-u))).astype(BF).astype(F32)
        left = jnp.where(col_index == 0, 0.0, pltpu.roll(u, 1, 0))
        right = jnp.where(col_index == W - 1, 0.0, pltpu.roll(u, W - 1, 0))
        act3[pl.ds(row * W, W), 0:D] = left.astype(BF)
        act3[pl.ds(row * W, W), D : 2 * D] = u.astype(BF)
        act3[pl.ds(row * W, W), 2 * D : 3 * D] = right.astype(BF)

    activate(1, vid[0:W])
    activate(2, vid[W:T])
    loads[2].wait()
    conv_acc[...] = vid[...].astype(F32) + dot(act3[W : 3 * W], cw[1])
    loads[3].wait()
    conv_acc[W:T] += dot(act3[W : 2 * W], cw[0])
    loads[4].wait()
    conv_acc[0:W] += dot(act3[2 * W : 3 * W], cw[2])

    @pl.when(has_up)
    def _():
        to_down.wait_recv()
        activate(0, halo[0])
        conv_acc[0:W] += dot(act3[0:W], cw[0])

    @pl.when(has_down)
    def _():
        to_up.wait_recv()
        activate(3, halo[1])
        conv_acc[W:T] += dot(act3[3 * W : 4 * W], cw[2])

    loads[5].wait()
    loads[6].wait()
    loads[7].wait()
    swap = pltpu.make_async_remote_copy(
        src_ref=ac_mine, dst_ref=ac_t, send_sem=swap_send, recv_sem=swap_recv,
        device_id=(col * 2 + 1 - c, (1 - h) * ZS + z), device_id_type=MESH,
    )

    @pl.when(stays)
    def _():
        ac_t[...] = conv_acc[...].astype(BF)

    @pl.when(jnp.logical_not(stays))
    def _():
        ac_mine[...] = conv_acc[...].astype(BF)
        swap.start()
        swap.wait_recv()

    nall[c, z] = channel_norm(ac_t[...].astype(F32), gs[...]).astype(BF)

    def origin(side, dist):
        return lax.rem(z + (ZS - dist if side == 0 else dist), ZS)

    def ring_piece(side, dist, part):
        ref = nall.at[c, origin(side, dist), pl.ds(part * HALF, HALF)]
        return pltpu.make_async_remote_copy(
            src_ref=ref, dst_ref=ref, send_sem=ring_send.at[side, dist, part], recv_sem=recv.at[c, side, dist + 1, part],
            device_id=z_ids[side], device_id_type=MESH,
        )

    def sib_piece(ring_core, side, dist, part):
        ref = nall.at[ring_core, origin(side, dist), pl.ds(part * HALF, HALF)]
        return pltpu.make_async_remote_copy(
            src_ref=ref, dst_ref=ref, send_sem=sib_send.at[side, dist, part], recv_sem=recv.at[ring_core, side, dist, part],
            device_id=sibling, device_id_type=MESH,
        )

    for part in range(2):
        for side in range(2):
            ring_piece(side, 0, part if side == 0 else 1 - part).start()
    for part in range(2):
        sib_piece(c, 0, 0, part).start()

    query = dot(nall[c, z], wq_v[...]).astype(BF)
    q_v[...] = (dot_t(query, wk_v[...]) * (SCALE * LOG2E)).astype(BF)
    m_v[...] = jnp.full(m_v.shape, -1e30, F32)
    l_v[...] = jnp.zeros(l_v.shape, F32)
    acc_v[...] = jnp.zeros(acc_v.shape, F32)

    def pieces(dist):
        if dist == 0:
            return [(0, 0), (0, 1)]
        if dist == ZS // 2:
            return [(0, 0), (1, 1)]
        return [(0, 0), (1, 1), (0, 1), (1, 0)]

    def arrive(ring, dist):
        ring_core = h if ring == 0 else 1 - h
        mine = ring_core == c
        for side, part in pieces(dist):
            wait = sib_piece(ring_core, side, dist, part)
            if dist == 0:
                @pl.when(jnp.logical_not(mine))
                def _():
                    wait.wait_recv()
                continue
            wait.wait_recv()

            @pl.when(mine)
            def _():
                if dist < ZS // 2 - 1 or (dist == ZS // 2 - 1 and side == part):
                    ring_piece(side, dist, part).start()
                sib_piece(c, side, dist, part).start()

    def attend(t, carry):
        for k, (ring, dist, side) in enumerate(ORDER):
            if side == 0:
                @pl.when(t == k)
                def _():
                    arrive(ring, dist)
        ring_t = pick(t, [r for r, _, _ in ORDER])
        off_t = pick(t, [(ZS - dist) % ZS if side == 0 else dist for _, dist, side in ORDER])
        ring_core = jnp.where(ring_t == 0, h, 1 - h)
        keys = nall[ring_core, lax.rem(z + off_t, ZS)]
        s = dot_t(q_v[...], keys)
        m_old = m_v[:, 0:1]
        m_new = jnp.maximum(m_old, jnp.max(s, axis=1, keepdims=True))
        p = jnp.exp2(s - m_new)
        alpha = jnp.exp2(m_old - m_new)
        l_v[...] = jnp.broadcast_to(l_v[:, 0:1] * alpha + jnp.sum(p, axis=1, keepdims=True), l_v.shape)
        m_v[...] = jnp.broadcast_to(m_new, m_v.shape)
        acc_v[...] = acc_v[...] * alpha + dot(p.astype(BF), keys)
        return carry

    lax.fori_loop(0, len(ORDER), attend, 0)

    loads[8].wait()
    loads[9].wait()
    mixed = (acc_v[...] / l_v[:, 0:1]).astype(BF)
    mixed = dot(mixed, wv_v[...]).astype(BF)
    as_t[...] = (ac_t[...].astype(F32) + dot(mixed, wo_v[...])).astype(BF)

    frame = col * 2 + h
    home = c * ZS + z

    def owner(j):
        i = j - TM
        return jnp.where(j < TM, j, i * 4 + lax.rem(i, 2) * 2)

    def a_piece(j, f):
        slot = j // TM
        return pltpu.make_async_remote_copy(
            src_ref=as_t.at[pl.ds(pl.multiple_of(j * PIECE, PIECE), PIECE)],
            dst_ref=tbuf.at[slot, pl.ds(pl.multiple_of(f * PIECE, PIECE), PIECE)],
            send_sem=a_send.at[j], recv_sem=a_recv.at[slot, f],
            device_id=(owner(j), home), device_id_type=MESH,
        )

    def a_local(j):
        slot = j // TM
        return pltpu.make_async_copy(
            as_t.at[pl.ds(pl.multiple_of(j * PIECE, PIECE), PIECE)],
            tbuf.at[slot, pl.ds(pl.multiple_of(frame * PIECE, PIECE), PIECE)],
            a_self.at[slot],
        )

    def is_me(j):
        return jnp.logical_and(stays, owner(j) == tm)

    def a_start(j, carry):
        @pl.when(is_me(j))
        def _():
            a_local(j).start()

        @pl.when(jnp.logical_not(is_me(j)))
        def _():
            a_piece(j, frame).start()

        return carry

    lax.fori_loop(0, PIECES, a_start, 0)
    second = tm // 4
    has_second = tm == second * 4 + lax.rem(second, 2) * 2
    for i in range(10, 15):
        loads[i].wait()

    rows = FRAMES * PIECE
    r_index = lax.broadcasted_iota(jnp.int32, (rows, rows), 0)
    c_index = lax.broadcasted_iota(jnp.int32, (rows, rows), 1)
    allowed = jnp.logical_and((r_index & (PIECE - 1)) == (c_index & (PIECE - 1)), r_index >= c_index)

    def d_piece(slot, j, f):
        return pltpu.make_async_remote_copy(
            src_ref=dbuf.at[slot, pl.ds(pl.multiple_of(f * PIECE, PIECE), PIECE)],
            dst_ref=out.at[pl.ds(pl.multiple_of(j * PIECE, PIECE), PIECE)],
            send_sem=d_send.at[slot, f], recv_sem=d_recv.at[j],
            device_id=(f, sp), device_id_type=MESH,
        )

    def d_local(slot, j):
        return pltpu.make_async_copy(
            dbuf.at[slot, pl.ds(pl.multiple_of(tm * PIECE, PIECE), PIECE)],
            out.at[pl.ds(pl.multiple_of(j * PIECE, PIECE), PIECE)],
            d_self.at[slot],
        )

    def temporal(slot, j):
        def wait_piece(f, carry):
            own = jnp.logical_and(stays, f == frame)

            @pl.when(own)
            def _():
                a_local(j).wait()

            @pl.when(jnp.logical_not(own))
            def _():
                a_piece(slot * TM, f).wait_recv()

            return carry

        lax.fori_loop(0, FRAMES, wait_piece, 0)
        x = tbuf[slot]
        normed = channel_norm(x.astype(F32), gt[...]).astype(BF)
        q = dot(normed, tq_v[...]).astype(BF)
        k = dot(normed, tk_v[...]).astype(BF)
        v = dot(normed, tv_v[...]).astype(BF)
        s = jnp.where(allowed, dot_t(q, k) * (SCALE * LOG2E), -1e30)
        p = jnp.exp2(s - jnp.max(s, axis=1, keepdims=True))
        total = jnp.sum(p, axis=1, keepdims=True)
        mix = (dot(p.astype(BF), v) / total).astype(BF)
        dbuf[slot] = (x.astype(F32) + dot(mix, to_v[...])).astype(BF)

        def d_start(f, carry):
            @pl.when(f == tm)
            def _():
                d_local(slot, j).start()

            @pl.when(f != tm)
            def _():
                d_piece(slot, j, f).start()

            return carry

        lax.fori_loop(0, FRAMES, d_start, 0)

    temporal(0, tm)

    @pl.when(has_second)
    def _():
        temporal(1, TM + second)

    def d_wait(j, carry):
        mine = owner(j) == tm

        @pl.when(mine)
        def _():
            d_local(j // TM, j).wait()

        @pl.when(jnp.logical_not(mine))
        def _():
            d_piece(0, j, tm).wait_recv()

        return carry

    lax.fori_loop(0, PIECES, d_wait, 0)

    def a_sent(j, carry):
        @pl.when(jnp.logical_not(is_me(j)))
        def _():
            a_piece(j, frame).wait_send()

        return carry

    lax.fori_loop(0, PIECES, a_sent, 0)

    def d_sent(f, carry):
        @pl.when(f != tm)
        def _():
            d_piece(0, tm, f).wait_send()

            @pl.when(has_second)
            def _():
                d_piece(1, tm, f).wait_send()

        return carry

    lax.fori_loop(0, FRAMES, d_sent, 0)

    @pl.when(has_down)
    def _():
        to_down.wait_send()

    @pl.when(has_up)
    def _():
        to_up.wait_send()

    @pl.when(jnp.logical_not(stays))
    def _():
        swap.wait_send()

    for dist in range(ZS // 2 + 1):
        for side, part in pieces(dist):
            sib_piece(c, side, dist, part).wait_send()
    for dist in range(ZS // 2):
        for side in range(2):
            for part in range(2):
                if dist < ZS // 2 - 1 or side == part:
                    ring_piece(side, dist, part).wait_send()


def local(
    video, gain_conv, conv_weight, gain_space, query_weight, key_weight, value_weight, out_weight,
    gain_time, time_query, time_key, time_value, time_out,
):
    vm = pltpu.VMEM
    dma = pltpu.SemaphoreType.DMA
    decoded = pl.pallas_call(
        kernel,
        out_shape=jax.ShapeDtypeStruct((T, D), BF),
        in_specs=[pl.BlockSpec(memory_space=pl.ANY)] * 13,
        out_specs=pl.BlockSpec(memory_space=pl.ANY),
        scratch_shapes=[
            vm((T, D), BF), vm((2, W, D), BF), vm((1, D), F32), vm((1, D), F32), vm((1, D), F32),
            vm((3, 3 * D, D), BF), *[vm((D, D), BF) for _ in range(8)],
            vm((4 * W, 3 * D), BF), vm((T, D), F32), vm((T, D), BF), vm((T, D), BF), vm((2, ZS, T, D), BF),
            vm((T, D), BF), vm((T, 128), F32), vm((T, 128), F32), vm((T, D), F32), vm((T, D), BF),
            vm((2, FRAMES * PIECE, D), BF), vm((2, FRAMES * PIECE, D), BF),
            dma((15,)), dma((2,)), dma((2,)), dma, dma,
            dma((2, 4, 2)), dma((2, 5, 2)), dma((2, 2, 5, 2)),
            dma((PIECES,)), dma((2, FRAMES)), dma((2,)), dma((2, FRAMES)), dma((PIECES,)), dma((2,)),
        ],
        compiler_params=pltpu.CompilerParams(
            collective_id=0, has_side_effects=True, vmem_limit_bytes=56 * 1024 * 1024
        ),
    )(
        video.reshape(T, D), gain_conv.reshape(1, D), conv_weight.reshape(3, 3 * D, D), gain_space.reshape(1, D),
        query_weight, key_weight, value_weight, out_weight, gain_time.reshape(1, D),
        time_query, time_key, time_value, time_out,
    )
    return decoded.reshape(1, 2, W, D)


def solution(mesh):
    return jax.shard_map(
        local,
        mesh=mesh,
        in_specs=(P("tm", "space", None, None),) + (P(),) * 12,
        out_specs=P("tm", "space", None, None),
        check_vma=False,
    )
```

time: 319 us -> 73.5 us (0.23)
  waiting for transfers between devices: 218 us -> 0 us
  Pallas kernels: 0 us -> 71.7 us
  matrix products: 22.8 us -> 0 us
  starting transfers between devices: 21.3 us -> 0 us
  other arithmetic: 18.4 us -> 0 us
  between operations: 13.9 us -> 0.01 us
  blocking collectives: 11.6 us -> 0 us
  local copies, waits for them, and re-layouts: 12.7 us -> 1.72 us
    all_gather x2 -> x0, waiting for transfers between devices: 203 us -> none  [the longest x1 107 us: local(): lax.all_gather(key_rows, 'space', axis=0, tiled=True)]
    pallas_call x0 -> x1, Pallas kernels: none -> 71.7 us  [local(): pl.pallas_call(kernel, out_shape=jax.ShapeDtypeStruct((T, D), BF), in_spe...]
    dot_general x19 -> x0, matrix products: 22.8 us -> none  [the longest x1 7.33 us: attend_block(): jnp.dot(query, key_rows.T, preferred_element_type=jnp.float32) * score_scale]
    all_to_all x3 -> x0, starting transfers between devices: 15.4 us -> none  [the longest x1 7.7 us: local(): lax.all_to_all(time_q, 'tm', split_axis=1, concat_axis=0, tiled=True)]
    all_to_all x1 -> x0, blocking collectives: 11.6 us -> none  [local(): lax.all_to_all(temporal, 'tm', split_axis=0, concat_axis=1, tiled=True)]
    all_to_all x3 -> x0, waiting for transfers between devices: 10.1 us -> none  [the longest x1 3.64 us: local(): lax.all_to_all(time_q, 'tm', split_axis=1, concat_axis=0, tiled=True)]
    unnamed x3 -> x0, other arithmetic: 7.96 us -> none
    reduce_sum x6 -> x0, other arithmetic: 7.25 us -> none  [the longest x1 3.95 us: attend_block(): totals = jnp.sum(expd, axis=1)]
  transfers between devices with their start and end apart: 7 -> 0, of which waited for: 7 -> 0; matrix products, arithmetic and copies ran while one was open for 8% -> 0% of each run, Pallas kernels for 0% -> 0%
where the time goes in v1:
time: 73.5 us; the launch traced here: 73.4 us
  Pallas kernels  71.7 us (98%)
  local copies, waits for them, and re-layouts  1.72 us (2%)
    pallas_call x1, Pallas kernels, local(): pl.pallas_call(kernel, out_shape=jax.ShapeDtypeStruct((T, D), BF), in_spe...  71.7 us
    unnamed x1, local copies, waits for them, and re-layouts  1.72 us

profile of v1, /device:TPU:1, one launch (start us, length us, event | category | flops | bytes accessed | tf_op | source)
XLA Modules:
  0.0 73.4 jit_solution(817483542222355307)
XLA Ops:
  0.0 71.7 %shard_map.127 = bf16[320,512]{1,0:T(8,128)(2,1)} custom-call(bf16[320,512]{1,0:T(8,128)(2,1)} %bitcast.8, f32[1,512]{1,0:T(1,128)} %bitcast.9, bf16[3,1536,512]{2,1,0:T(8,128)(2,1)} %bitcast.6, f32[1,512]{1,0:T(1,128)} %bitcast.10, bf16[512,512]{1,0:T(8,128)(2,1)} %wq.1, bf16[512,512]{1,0:T(8,128)(2,1)} %wk.1, bf16[512,512]{1,0:T(8,128)(2,1)} %wv.1, ...), custom_call_target="tpu_custom_call" | custom-call | tf_op jit(solution)/shard_map/pallas_call | solution.py:448
  71.7 1.7 %copy.15 = bf16[1,2,160,512]{3,2,1,0:T(8,128)(2,1)} copy(bf16[1,2,160,512]{3,2,1,0:T(8,128)(2,1)} %bitcast.7) | data formatting | bytes 655360

commit v2 on v1

--- a/solution.py
+++ b/solution.py
@@ -23,9 +23,9 @@
 BF = jnp.bfloat16
 F32 = jnp.float32
 
-ORDER = [(0, 0, 0)]
-for ring, dist in [(0, 1), (1, 0), (0, 2), (1, 1), (0, 3), (1, 2), (0, 4), (1, 3), (1, 4)]:
-    ORDER += [(ring, dist, 0)] if dist in (0, 4) else [(ring, dist, 0), (ring, dist, 1)]
+QUARTER = T // 4
+KEYS = 2 * T
+STEPS = ZS * 2 * T // KEYS
 
 
 def channel_norm(values, gains):
@@ -47,21 +47,13 @@
     return i * 4 + (i % 2) * 2
 
 
-def pick(t, values):
-    out = jnp.int32(values[0])
-    for k, v in enumerate(values):
-        if k:
-            out = jnp.where(t == k, jnp.int32(v), out)
-    return out
-
-
 def kernel(
     video, gain_conv, conv_w, gain_space, wq, wk, wv, wo, gain_time, tq, tk, tv, to,
     out,
     vid, halo, gc, gs, gt, cw, wq_v, wk_v, wv_v, wo_v, tq_v, tk_v, tv_v, to_v,
-    act3, conv_acc, ac_mine, ac_t, nall, q_v, m_v, l_v, acc_v, as_t, tbuf, dbuf,
+    act3, conv_acc, ac_t, nall, q_v, m_v, l_v, acc_v, as_t, tbuf, dbuf,
     load_sem, halo_send, halo_recv, swap_send, swap_recv,
-    ring_send, sib_send, recv,
+    ring_send, ring_recv, sib_send, sib_recv,
     a_send, a_recv, a_self, d_send, d_recv, d_self,
 ):
     tm = lax.axis_index("tm")
@@ -75,11 +67,13 @@
     sibling = (col * 2 + 1 - c, sp)
     z_ids = ((tm, h * ZS + zp), (tm, h * ZS + zm))
     stays = c == h
+    block = c * ZS + z
+    last = YH * ZS - 1
 
     loads = []
     for i, (src, dst) in enumerate(
         [
-            (video, vid), (gain_conv, gc), (conv_w.at[1], cw.at[1]), (conv_w.at[0], cw.at[0]),
+            (gain_conv, gc), (conv_w.at[1], cw.at[1]), (conv_w.at[0], cw.at[0]),
             (conv_w.at[2], cw.at[2]), (gain_space, gs), (wq, wq_v), (wk, wk_v), (wv, wv_v), (wo, wo_v),
             (gain_time, gt), (tq, tq_v), (tk, tk_v), (tv, tv_v), (to, to_v),
         ]
@@ -87,6 +81,12 @@
         loads.append(pltpu.make_async_copy(src, dst, load_sem.at[i]))
         loads[-1].start()
 
+    own_load = pltpu.make_async_copy(video, vid, load_sem.at[14])
+
+    @pl.when(stays)
+    def _():
+        own_load.start()
+
     barrier = pltpu.get_barrier_semaphore()
 
     def greet(i, carry):
@@ -100,43 +100,59 @@
         return carry
 
     lax.fori_loop(0, TM * YH, greet, 0)
-    for target in z_ids:
-        pl.semaphore_signal(barrier, inc=1, device_id=target, device_id_type=MESH)
-    crosses_down = sp == ZS - 1
-    crosses_up = sp == ZS
-
-    @pl.when(crosses_down)
-    def _():
-        pl.semaphore_signal(barrier, inc=1, device_id=(tm, ZS), device_id_type=MESH)
-
-    @pl.when(crosses_up)
-    def _():
-        pl.semaphore_signal(barrier, inc=1, device_id=(tm, ZS - 1), device_id_type=MESH)
-
-    crosses = jnp.where(jnp.logical_or(crosses_down, crosses_up), 1, 0)
-    pl.semaphore_wait(barrier, TM * YH - 1 + 2 + crosses)
-
-    has_up = sp > 0
-    has_down = sp < YH * ZS - 1
+
+    def greet_z(i, carry):
+        for other_z in (zp, zm):
+            other = (col * 2 + lax.rem(i, 2), (i // 2) * ZS + other_z)
+            pl.semaphore_signal(barrier, inc=1, device_id=other, device_id_type=MESH)
+        return carry
+
+    lax.fori_loop(0, CORES * YH, greet_z, 0)
+    pl.semaphore_wait(barrier, TM * YH - 1 + 2 * CORES * YH)
+
+    def place(s):
+        return (col * 2 + lax.div(s, ZS), c * ZS + lax.rem(s, ZS))
+
+    sends_down = sp < last
+    sends_up = sp > 0
+    gets_down = block > 0
+    gets_up = block < last
     to_down = pltpu.make_async_remote_copy(
         src_ref=video.at[pl.ds(W, W)], dst_ref=halo.at[0], send_sem=halo_send.at[0], recv_sem=halo_recv.at[0],
-        device_id=(tm, jnp.minimum(sp + 1, YH * ZS - 1)), device_id_type=MESH,
+        device_id=place(jnp.minimum(sp + 1, last)), device_id_type=MESH,
     )
     to_up = pltpu.make_async_remote_copy(
         src_ref=video.at[pl.ds(0, W)], dst_ref=halo.at[1], send_sem=halo_send.at[1], recv_sem=halo_recv.at[1],
-        device_id=(tm, jnp.maximum(sp - 1, 0)), device_id_type=MESH,
+        device_id=place(jnp.maximum(sp - 1, 0)), device_id_type=MESH,
     )
-
-    @pl.when(has_down)
+    swap = pltpu.make_async_remote_copy(
+        src_ref=video, dst_ref=vid, send_sem=swap_send, recv_sem=swap_recv,
+        device_id=place(sp), device_id_type=MESH,
+    )
+
+    away = jnp.logical_not(stays)
+
+    @pl.when(away)
+    def _():
+        swap.start()
+
+    @pl.when(sends_down)
     def _():
         to_down.start()
 
-    @pl.when(has_up)
+    @pl.when(sends_up)
     def _():
         to_up.start()
 
+    @pl.when(stays)
+    def _():
+        own_load.wait()
+
+    @pl.when(away)
+    def _():
+        swap.wait_recv()
+
     loads[0].wait()
-    loads[1].wait()
     col_index = lax.broadcasted_iota(jnp.int32, (W, D), 0)
 
     def activate(row, raw):
@@ -150,109 +166,131 @@
 
     activate(1, vid[0:W])
     activate(2, vid[W:T])
+    loads[1].wait()
+    conv_acc[...] = vid[...].astype(F32) + dot(act3[W : 3 * W], cw[1])
     loads[2].wait()
-    conv_acc[...] = vid[...].astype(F32) + dot(act3[W : 3 * W], cw[1])
+    conv_acc[W:T] += dot(act3[W : 2 * W], cw[0])
     loads[3].wait()
-    conv_acc[W:T] += dot(act3[W : 2 * W], cw[0])
-    loads[4].wait()
     conv_acc[0:W] += dot(act3[2 * W : 3 * W], cw[2])
 
-    @pl.when(has_up)
+    @pl.when(gets_down)
     def _():
         to_down.wait_recv()
         activate(0, halo[0])
         conv_acc[0:W] += dot(act3[0:W], cw[0])
 
-    @pl.when(has_down)
+    @pl.when(gets_up)
     def _():
         to_up.wait_recv()
         activate(3, halo[1])
         conv_acc[W:T] += dot(act3[3 * W : 4 * W], cw[2])
 
-    loads[5].wait()
-    loads[6].wait()
-    loads[7].wait()
-    swap = pltpu.make_async_remote_copy(
-        src_ref=ac_mine, dst_ref=ac_t, send_sem=swap_send, recv_sem=swap_recv,
-        device_id=(col * 2 + 1 - c, (1 - h) * ZS + z), device_id_type=MESH,
-    )
-
-    @pl.when(stays)
-    def _():
-        ac_t[...] = conv_acc[...].astype(BF)
-
-    @pl.when(jnp.logical_not(stays))
-    def _():
-        ac_mine[...] = conv_acc[...].astype(BF)
-        swap.start()
-        swap.wait_recv()
-
-    nall[c, z] = channel_norm(ac_t[...].astype(F32), gs[...]).astype(BF)
-
-    def origin(side, dist):
-        return lax.rem(z + (ZS - dist if side == 0 else dist), ZS)
+    loads[4].wait()
+    after_conv = conv_acc[...].astype(BF)
+    ac_t[...] = after_conv
+
+    my_ring = jnp.where(stays, 0, 1)
+
+    def place_of(ring, side, dist):
+        if dist == 0:
+            return ring * T
+        if dist == ZS // 2:
+            return (4 * dist - 2 + ring) * T
+        return (4 * dist - 2 + 2 * ring + side) * T
+
+    def rows_of(ring, side, dist, start, size):
+        return nall.at[pl.ds(pl.multiple_of(place_of(ring, side, dist) + start, PIECE), size)]
+
+    nall[pl.ds(pl.multiple_of(my_ring * T, T), T)] = channel_norm(after_conv.astype(F32), gs[...]).astype(BF)
 
     def ring_piece(side, dist, part):
-        ref = nall.at[c, origin(side, dist), pl.ds(part * HALF, HALF)]
         return pltpu.make_async_remote_copy(
-            src_ref=ref, dst_ref=ref, send_sem=ring_send.at[side, dist, part], recv_sem=recv.at[c, side, dist + 1, part],
+            src_ref=rows_of(my_ring, side, dist, part * QUARTER, QUARTER),
+            dst_ref=rows_of(my_ring, side, dist + 1, part * QUARTER, QUARTER),
+            send_sem=ring_send.at[side, dist, part], recv_sem=ring_recv.at[side, dist, part],
             device_id=z_ids[side], device_id_type=MESH,
         )
 
-    def sib_piece(ring_core, side, dist, part):
-        ref = nall.at[ring_core, origin(side, dist), pl.ds(part * HALF, HALF)]
+    def sib_piece(ring, side, dist, half):
+        ref = rows_of(ring, side, dist, half * HALF, HALF)
         return pltpu.make_async_remote_copy(
-            src_ref=ref, dst_ref=ref, send_sem=sib_send.at[side, dist, part], recv_sem=recv.at[ring_core, side, dist, part],
+            src_ref=ref, dst_ref=ref, send_sem=sib_send.at[side, dist, half], recv_sem=sib_recv.at[side, dist, half],
             device_id=sibling, device_id_type=MESH,
         )
 
-    for part in range(2):
+    parts = ((0, 1, 2, 3), (2, 3, 0, 1))
+
+    def travels(side, dist, part):
+        return dist < ZS // 2 - 1 or (dist == ZS // 2 - 1 and part // 2 == side)
+
+    def halves(side, dist):
+        if dist == 0:
+            return (0, 1) if side == 0 else ()
+        return (side, 1 - side) if dist < ZS // 2 else (side,)
+
+    for i in range(4):
         for side in range(2):
-            ring_piece(side, 0, part if side == 0 else 1 - part).start()
-    for part in range(2):
-        sib_piece(c, 0, 0, part).start()
-
-    query = dot(nall[c, z], wq_v[...]).astype(BF)
+            ring_piece(side, 0, parts[side][i]).start()
+    for half in range(2):
+        sib_piece(my_ring, 0, 0, half).start()
+
+    loads[5].wait()
+    query = dot(nall[pl.ds(pl.multiple_of(my_ring * T, T), T)], wq_v[...]).astype(BF)
+    loads[6].wait()
     q_v[...] = (dot_t(query, wk_v[...]) * (SCALE * LOG2E)).astype(BF)
     m_v[...] = jnp.full(m_v.shape, -1e30, F32)
     l_v[...] = jnp.zeros(l_v.shape, F32)
     acc_v[...] = jnp.zeros(acc_v.shape, F32)
 
-    def pieces(dist):
-        if dist == 0:
-            return [(0, 0), (0, 1)]
-        if dist == ZS // 2:
-            return [(0, 0), (1, 1)]
-        return [(0, 0), (1, 1), (0, 1), (1, 0)]
-
-    def arrive(ring, dist):
-        ring_core = h if ring == 0 else 1 - h
-        mine = ring_core == c
-        for side, part in pieces(dist):
-            wait = sib_piece(ring_core, side, dist, part)
-            if dist == 0:
-                @pl.when(jnp.logical_not(mine))
-                def _():
-                    wait.wait_recv()
-                continue
-            wait.wait_recv()
-
-            @pl.when(mine)
-            def _():
-                if dist < ZS // 2 - 1 or (dist == ZS // 2 - 1 and side == part):
+    def own(dist, half):
+        if dist == ZS // 2 and half == 1:
+            return
+        for i in (2 * half, 2 * half + 1):
+            for side in range(2):
+                part = parts[side][i]
+                ring_piece(side, dist - 1, part).wait_recv()
+                if travels(side, dist, part):
                     ring_piece(side, dist, part).start()
-                sib_piece(c, side, dist, part).start()
+        for side in range(2):
+            sib_piece(my_ring, side, dist, halves(side, dist)[half]).start()
+
+    def other(dist):
+        for side in range(2):
+            for half in halves(side, dist):
+                sib_piece(1 - my_ring, side, dist, half).wait_recv()
+
+    def first_ring(t):
+        if t == 0:
+            own(1, 0)
+            other(0)
+        elif t % 2 == 1:
+            own((t + 1) // 2, 1)
+            if t == STEPS - 1:
+                other(ZS // 2)
+        else:
+            own(t // 2 + 1, 0)
+            other(t // 2)
+
+    def second_ring(t):
+        if t == 0:
+            other(0)
+        elif t % 2 == 1:
+            own((t + 1) // 2, 0)
+            other((t + 1) // 2)
+        else:
+            own(t // 2, 1)
 
     def attend(t, carry):
-        for k, (ring, dist, side) in enumerate(ORDER):
-            if side == 0:
-                @pl.when(t == k)
-                def _():
-                    arrive(ring, dist)
-        ring_t = pick(t, [r for r, _, _ in ORDER])
-        off_t = pick(t, [(ZS - dist) % ZS if side == 0 else dist for _, dist, side in ORDER])
-        ring_core = jnp.where(ring_t == 0, h, 1 - h)
-        keys = nall[ring_core, lax.rem(z + off_t, ZS)]
+        for k in range(STEPS):
+            @pl.when(jnp.logical_and(t == k, stays))
+            def _():
+                first_ring(k)
+
+            @pl.when(jnp.logical_and(t == k, away))
+            def _():
+                second_ring(k)
+
+        keys = nall[pl.ds(pl.multiple_of(t * KEYS, KEYS), KEYS)]
         s = dot_t(q_v[...], keys)
         m_old = m_v[:, 0:1]
         m_new = jnp.maximum(m_old, jnp.max(s, axis=1, keepdims=True))
@@ -263,10 +301,10 @@
         acc_v[...] = acc_v[...] * alpha + dot(p.astype(BF), keys)
         return carry
 
-    lax.fori_loop(0, len(ORDER), attend, 0)
-
+    lax.fori_loop(0, STEPS, attend, 0)
+
+    loads[7].wait()
     loads[8].wait()
-    loads[9].wait()
     mixed = (acc_v[...] / l_v[:, 0:1]).astype(BF)
     mixed = dot(mixed, wv_v[...]).astype(BF)
     as_t[...] = (ac_t[...].astype(F32) + dot(mixed, wo_v[...])).astype(BF)
@@ -312,7 +350,7 @@
     lax.fori_loop(0, PIECES, a_start, 0)
     second = tm // 4
     has_second = tm == second * 4 + lax.rem(second, 2) * 2
-    for i in range(10, 15):
+    for i in range(9, 14):
         loads[i].wait()
 
     rows = FRAMES * PIECE
@@ -417,25 +455,24 @@
 
     lax.fori_loop(0, FRAMES, d_sent, 0)
 
-    @pl.when(has_down)
+    @pl.when(sends_down)
     def _():
         to_down.wait_send()
 
-    @pl.when(has_up)
+    @pl.when(sends_up)
     def _():
         to_up.wait_send()
 
-    @pl.when(jnp.logical_not(stays))
+    @pl.when(away)
     def _():
         swap.wait_send()
 
     for dist in range(ZS // 2 + 1):
-        for side, part in pieces(dist):
-            sib_piece(c, side, dist, part).wait_send()
-    for dist in range(ZS // 2):
         for side in range(2):
-            for part in range(2):
-                if dist < ZS // 2 - 1 or side == part:
+            for half in halves(side, dist):
+                sib_piece(my_ring, side, dist, half).wait_send()
+            for part in parts[side]:
+                if travels(side, dist, part):
                     ring_piece(side, dist, part).wait_send()
 
 
@@ -453,11 +490,11 @@
         scratch_shapes=[
             vm((T, D), BF), vm((2, W, D), BF), vm((1, D), F32), vm((1, D), F32), vm((1, D), F32),
             vm((3, 3 * D, D), BF), *[vm((D, D), BF) for _ in range(8)],
-            vm((4 * W, 3 * D), BF), vm((T, D), F32), vm((T, D), BF), vm((T, D), BF), vm((2, ZS, T, D), BF),
+            vm((4 * W, 3 * D), BF), vm((T, D), F32), vm((T, D), BF), vm((2 * ZS * T, D), BF),
             vm((T, D), BF), vm((T, 128), F32), vm((T, 128), F32), vm((T, D), F32), vm((T, D), BF),
             vm((2, FRAMES * PIECE, D), BF), vm((2, FRAMES * PIECE, D), BF),
             dma((15,)), dma((2,)), dma((2,)), dma, dma,
-            dma((2, 4, 2)), dma((2, 5, 2)), dma((2, 2, 5, 2)),
+            dma((2, 4, 4)), dma((2, 4, 4)), dma((2, 5, 2)), dma((2, 5, 2)),
             dma((PIECES,)), dma((2, FRAMES)), dma((2,)), dma((2, FRAMES)), dma((PIECES,)), dma((2,)),
         ],
         compiler_params=pltpu.CompilerParams(

time: 73.5 us -> 66.9 us (0.910)
  Pallas kernels: 71.7 us -> 65.1 us
    pallas_call x1, Pallas kernels: 71.7 us -> 65.1 us  [local(): pl.pallas_call(kernel, out_shape=jax.ShapeDtypeStruct((T, D), BF), in_spe...]
where the time goes in v2:
time: 66.9 us; the launch traced here: 66.8 us
  Pallas kernels  65.1 us (97%)
  local copies, waits for them, and re-layouts  1.72 us (3%)
    pallas_call x1, Pallas kernels, local(): pl.pallas_call(kernel, out_shape=jax.ShapeDtypeStruct((T, D), BF), in_spe...  65.1 us
    unnamed x1, local copies, waits for them, and re-layouts  1.72 us

profile of v2, /device:TPU:1, one launch (start us, length us, event | category | flops | bytes accessed | tf_op | source)
XLA Modules:
  0.0 66.8 jit_solution(2464811192285068519)
XLA Ops:
  0.0 65.1 %shard_map.127 = bf16[320,512]{1,0:T(8,128)(2,1)} custom-call(bf16[320,512]{1,0:T(8,128)(2,1)} %bitcast.8, f32[1,512]{1,0:T(1,128)} %bitcast.9, bf16[3,1536,512]{2,1,0:T(8,128)(2,1)} %bitcast.6, f32[1,512]{1,0:T(1,128)} %bitcast.10, bf16[512,512]{1,0:T(8,128)(2,1)} %wq.1, bf16[512,512]{1,0:T(8,128)(2,1)} %wk.1, bf16[512,512]{1,0:T(8,128)(2,1)} %wv.1, ...), custom_call_target="tpu_custom_call" | custom-call | tf_op jit(solution)/shard_map/pallas_call | solution.py:485
  65.1 1.7 %copy.15 = bf16[1,2,160,512]{3,2,1,0:T(8,128)(2,1)} copy(bf16[1,2,160,512]{3,2,1,0:T(8,128)(2,1)} %bitcast.7) | data formatting | bytes 655360

commit v3 on v2

--- a/solution.py
+++ b/solution.py
@@ -1,3 +1,4 @@
+import functools
 import math
 
 import jax
@@ -43,14 +44,14 @@
     return lax.dot_general(a, b, (((1,), (1,)), ((), ())), preferred_element_type=F32)
 
 
-def second_owner(i):
-    return i * 4 + (i % 2) * 2
+def owner(j):
+    return lax.rem(5 * j, TM)
 
 
 def kernel(
     video, gain_conv, conv_w, gain_space, wq, wk, wv, wo, gain_time, tq, tk, tv, to,
     out,
-    vid, halo, gc, gs, gt, cw, wq_v, wk_v, wv_v, wo_v, tq_v, tk_v, tv_v, to_v,
+    vid, halo, gc, gs, gt, cw, wq_v, wk_v, wv_v, wo_v, tq_v, tk_v, tv_v, to_v, wvo, tw,
     act3, conv_acc, ac_t, nall, q_v, m_v, l_v, acc_v, as_t, tbuf, dbuf,
     load_sem, halo_send, halo_recv, swap_send, swap_recv,
     ring_send, ring_recv, sib_send, sib_recv,
@@ -173,22 +174,6 @@
     loads[3].wait()
     conv_acc[0:W] += dot(act3[2 * W : 3 * W], cw[2])
 
-    @pl.when(gets_down)
-    def _():
-        to_down.wait_recv()
-        activate(0, halo[0])
-        conv_acc[0:W] += dot(act3[0:W], cw[0])
-
-    @pl.when(gets_up)
-    def _():
-        to_up.wait_recv()
-        activate(3, halo[1])
-        conv_acc[W:T] += dot(act3[3 * W : 4 * W], cw[2])
-
-    loads[4].wait()
-    after_conv = conv_acc[...].astype(BF)
-    ac_t[...] = after_conv
-
     my_ring = jnp.where(stays, 0, 1)
 
     def place_of(ring, side, dist):
@@ -200,8 +185,6 @@
 
     def rows_of(ring, side, dist, start, size):
         return nall.at[pl.ds(pl.multiple_of(place_of(ring, side, dist) + start, PIECE), size)]
-
-    nall[pl.ds(pl.multiple_of(my_ring * T, T), T)] = channel_norm(after_conv.astype(F32), gs[...]).astype(BF)
 
     def ring_piece(side, dist, part):
         return pltpu.make_async_remote_copy(
@@ -228,16 +211,37 @@
             return (0, 1) if side == 0 else ()
         return (side, 1 - side) if dist < ZS // 2 else (side,)
 
-    for i in range(4):
-        for side in range(2):
-            ring_piece(side, 0, parts[side][i]).start()
-    for half in range(2):
-        sib_piece(my_ring, 0, 0, half).start()
+    def finish_row(row, arrives, copy, tap):
+        part = slice(row * W, (row + 1) * W)
+
+        @pl.when(arrives)
+        def _():
+            copy.wait_recv()
+            activate(3 * row, halo[row])
+            conv_acc[part] += dot(act3[3 * row * W : (3 * row + 1) * W], cw[tap])
+
+        after_conv = conv_acc[part].astype(BF)
+        ac_t[part] = after_conv
+        at = pl.multiple_of(my_ring * T + row * W, PIECE)
+        nall[pl.ds(at, W)] = channel_norm(after_conv.astype(F32), gs[...]).astype(BF)
+        for quarter in (2 * row, 2 * row + 1):
+            for side in range(2):
+                ring_piece(side, 0, quarter).start()
+        sib_piece(my_ring, 0, 0, row).start()
+
+    loads[4].wait()
+    finish_row(0, gets_down, to_down, 0)
+    finish_row(1, gets_up, to_up, 2)
 
     loads[5].wait()
     query = dot(nall[pl.ds(pl.multiple_of(my_ring * T, T), T)], wq_v[...]).astype(BF)
     loads[6].wait()
     q_v[...] = (dot_t(query, wk_v[...]) * (SCALE * LOG2E)).astype(BF)
+    for i in range(7, 14):
+        loads[i].wait()
+    wvo[...] = dot(wv_v[...], wo_v[...]).astype(BF)
+    tw[:, 0:D] = (dot_t(tq_v[...], tk_v[...]) * (SCALE * LOG2E)).astype(BF)
+    tw[:, D : 2 * D] = dot(tv_v[...], to_v[...]).astype(BF)
     m_v[...] = jnp.full(m_v.shape, -1e30, F32)
     l_v[...] = jnp.zeros(l_v.shape, F32)
     acc_v[...] = jnp.zeros(acc_v.shape, F32)
@@ -259,62 +263,61 @@
             for half in halves(side, dist):
                 sib_piece(1 - my_ring, side, dist, half).wait_recv()
 
-    def first_ring(t):
-        if t == 0:
-            own(1, 0)
-            other(0)
-        elif t % 2 == 1:
-            own((t + 1) // 2, 1)
-            if t == STEPS - 1:
-                other(ZS // 2)
-        else:
-            own(t // 2 + 1, 0)
-            other(t // 2)
-
-    def second_ring(t):
-        if t == 0:
-            other(0)
-        elif t % 2 == 1:
-            own((t + 1) // 2, 0)
-            other((t + 1) // 2)
-        else:
-            own(t // 2, 1)
+    order_0 = (1, 0, 3, 2, 5, 4, 6, 7)
+    order_1 = (0, 1, 2, 3, 4, 5, 6, 7)
+    before_0 = (
+        lambda: (own(1, 0), own(1, 1)),
+        lambda: (own(2, 0), other(0)),
+        lambda: own(2, 1),
+        lambda: (own(3, 0), other(1)),
+        lambda: own(3, 1),
+        lambda: (own(4, 0), other(2)),
+        lambda: other(3),
+        lambda: other(4),
+    )
+    before_1 = (
+        lambda: other(0),
+        lambda: other(1),
+        lambda: (own(1, 0), own(1, 1)),
+        lambda: (own(2, 0), other(2)),
+        lambda: own(2, 1),
+        lambda: (own(3, 0), other(3)),
+        lambda: own(3, 1),
+        lambda: (own(4, 0), other(4)),
+    )
+
+    def arrive(k):
+        @pl.when(stays)
+        def _():
+            before_0[k]()
+
+        @pl.when(away)
+        def _():
+            before_1[k]()
 
     def attend(t, carry):
-        for k in range(STEPS):
-            @pl.when(jnp.logical_and(t == k, stays))
-            def _():
-                first_ring(k)
-
-            @pl.when(jnp.logical_and(t == k, away))
-            def _():
-                second_ring(k)
-
-        keys = nall[pl.ds(pl.multiple_of(t * KEYS, KEYS), KEYS)]
-        s = dot_t(q_v[...], keys)
-        m_old = m_v[:, 0:1]
+        index = jnp.int32(0)
+        for k in range(STEPS - 1):
+            pl.when(t == k)(functools.partial(arrive, k))
+            index = jnp.where(t == k, jnp.where(stays, order_0[k], order_1[k]), index)
+        attend_rows(slice(0, T), nall[pl.ds(pl.multiple_of(index * KEYS, KEYS), KEYS)])
+        return carry
+
+    def attend_rows(rows, keys):
+        s = dot_t(q_v[rows], keys)
+        m_old = m_v[rows, 0:1]
         m_new = jnp.maximum(m_old, jnp.max(s, axis=1, keepdims=True))
         p = jnp.exp2(s - m_new)
         alpha = jnp.exp2(m_old - m_new)
-        l_v[...] = jnp.broadcast_to(l_v[:, 0:1] * alpha + jnp.sum(p, axis=1, keepdims=True), l_v.shape)
-        m_v[...] = jnp.broadcast_to(m_new, m_v.shape)
-        acc_v[...] = acc_v[...] * alpha + dot(p.astype(BF), keys)
-        return carry
-
-    lax.fori_loop(0, STEPS, attend, 0)
-
-    loads[7].wait()
-    loads[8].wait()
-    mixed = (acc_v[...] / l_v[:, 0:1]).astype(BF)
-    mixed = dot(mixed, wv_v[...]).astype(BF)
-    as_t[...] = (ac_t[...].astype(F32) + dot(mixed, wo_v[...])).astype(BF)
+        l_new = l_v[rows, 0:1] * alpha + jnp.sum(p, axis=1, keepdims=True)
+        l_v[rows] = jnp.broadcast_to(l_new, (l_new.shape[0], 128))
+        m_v[rows] = jnp.broadcast_to(m_new, (l_new.shape[0], 128))
+        acc_v[rows] = acc_v[rows] * alpha + dot(p.astype(BF), keys)
+
+    lax.fori_loop(0, STEPS - 1, attend, 0)
 
     frame = col * 2 + h
     home = c * ZS + z
-
-    def owner(j):
-        i = j - TM
-        return jnp.where(j < TM, j, i * 4 + lax.rem(i, 2) * 2)
 
     def a_piece(j, f):
         slot = j // TM
@@ -347,11 +350,17 @@
 
         return carry
 
-    lax.fori_loop(0, PIECES, a_start, 0)
-    second = tm // 4
-    has_second = tm == second * 4 + lax.rem(second, 2) * 2
-    for i in range(9, 14):
-        loads[i].wait()
+    arrive(STEPS - 1)
+
+    for half in range(2):
+        part = slice(half * HALF, (half + 1) * HALF)
+        attend_rows(part, nall[(STEPS - 1) * KEYS :])
+        mixed = (acc_v[part] / l_v[part, 0:1]).astype(BF)
+        as_t[part] = (ac_t[part].astype(F32) + dot(mixed, wvo[...])).astype(BF)
+        lax.fori_loop(half * (PIECES // 2), (half + 1) * (PIECES // 2), a_start, 0)
+
+    first = lax.rem(13 * tm, TM)
+    has_second = first < PIECES - TM
 
     rows = FRAMES * PIECE
     r_index = lax.broadcasted_iota(jnp.int32, (rows, rows), 0)
@@ -390,14 +399,11 @@
         lax.fori_loop(0, FRAMES, wait_piece, 0)
         x = tbuf[slot]
         normed = channel_norm(x.astype(F32), gt[...]).astype(BF)
-        q = dot(normed, tq_v[...]).astype(BF)
-        k = dot(normed, tk_v[...]).astype(BF)
-        v = dot(normed, tv_v[...]).astype(BF)
-        s = jnp.where(allowed, dot_t(q, k) * (SCALE * LOG2E), -1e30)
+        qv = dot(normed, tw[...]).astype(BF)
+        s = jnp.where(allowed, dot_t(qv[:, 0:D], normed), -1e30)
         p = jnp.exp2(s - jnp.max(s, axis=1, keepdims=True))
         total = jnp.sum(p, axis=1, keepdims=True)
-        mix = (dot(p.astype(BF), v) / total).astype(BF)
-        dbuf[slot] = (x.astype(F32) + dot(mix, to_v[...])).astype(BF)
+        dbuf[slot] = (x.astype(F32) + dot(p.astype(BF), qv[:, D:]) / total).astype(BF)
 
         def d_start(f, carry):
             @pl.when(f == tm)
@@ -412,11 +418,11 @@
 
         lax.fori_loop(0, FRAMES, d_start, 0)
 
-    temporal(0, tm)
+    temporal(0, first)
 
     @pl.when(has_second)
     def _():
-        temporal(1, TM + second)
+        temporal(1, TM + first)
 
     def d_wait(j, carry):
         mine = owner(j) == tm
@@ -489,7 +495,7 @@
         out_specs=pl.BlockSpec(memory_space=pl.ANY),
         scratch_shapes=[
             vm((T, D), BF), vm((2, W, D), BF), vm((1, D), F32), vm((1, D), F32), vm((1, D), F32),
-            vm((3, 3 * D, D), BF), *[vm((D, D), BF) for _ in range(8)],
+            vm((3, 3 * D, D), BF), *[vm((D, D), BF) for _ in range(9)], vm((D, 2 * D), BF),
             vm((4 * W, 3 * D), BF), vm((T, D), F32), vm((T, D), BF), vm((2 * ZS * T, D), BF),
             vm((T, D), BF), vm((T, 128), F32), vm((T, 128), F32), vm((T, D), F32), vm((T, D), BF),
             vm((2, FRAMES * PIECE, D), BF), vm((2, FRAMES * PIECE, D), BF),

time: 66.9 us -> 63.7 us (0.952)
  Pallas kernels: 65.1 us -> 61.9 us
    pallas_call x1, Pallas kernels: 65.1 us -> 61.9 us  [local(): pl.pallas_call(kernel, out_shape=jax.ShapeDtypeStruct((T, D), BF), in_spe...]
where the time goes in v3:
time: 63.7 us; the launch traced here: 63.6 us
  Pallas kernels  61.9 us (97%)
  local copies, waits for them, and re-layouts  1.72 us (3%)
    pallas_call x1, Pallas kernels, local(): pl.pallas_call(kernel, out_shape=jax.ShapeDtypeStruct((T, D), BF), in_spe...  61.9 us
    unnamed x1, local copies, waits for them, and re-layouts  1.72 us

profile of v3, /device:TPU:1, one launch (start us, length us, event | category | flops | bytes accessed | tf_op | source)
XLA Modules:
  0.0 63.6 jit_solution(834940895631271087)
XLA Ops:
  0.0 61.9 %shard_map.127 = bf16[320,512]{1,0:T(8,128)(2,1)} custom-call(bf16[320,512]{1,0:T(8,128)(2,1)} %bitcast.8, f32[1,512]{1,0:T(1,128)} %bitcast.9, bf16[3,1536,512]{2,1,0:T(8,128)(2,1)} %bitcast.6, f32[1,512]{1,0:T(1,128)} %bitcast.10, bf16[512,512]{1,0:T(8,128)(2,1)} %wq.1, bf16[512,512]{1,0:T(8,128)(2,1)} %wk.1, bf16[512,512]{1,0:T(8,128)(2,1)} %wv.1, ...), custom_call_target="tpu_custom_call" | custom-call | tf_op jit(solution)/shard_map/pallas_call | solution.py:491
  61.9 1.7 %copy.15 = bf16[1,2,160,512]{3,2,1,0:T(8,128)(2,1)} copy(bf16[1,2,160,512]{3,2,1,0:T(8,128)(2,1)} %bitcast.7) | data formatting | bytes 655360

commit v4 on v3

--- a/solution.py
+++ b/solution.py
@@ -51,11 +51,11 @@
 def kernel(
     video, gain_conv, conv_w, gain_space, wq, wk, wv, wo, gain_time, tq, tk, tv, to,
     out,
-    vid, halo, gc, gs, gt, cw, wq_v, wk_v, wv_v, wo_v, tq_v, tk_v, tv_v, to_v, wvo, tw,
-    act3, conv_acc, ac_t, nall, q_v, m_v, l_v, acc_v, as_t, tbuf, dbuf,
+    vid, halo, gc, gs, gt, cw, wq_v, wk_v, wv_v, wo_v, tq_v, tk_v, tv_v, to_v, wvo, tw, tn, tv_n,
+    act3, conv_acc, ac_mine, ac_t, n_out, nall, q_v, m_v, l_v, acc_v, as_t, tbuf, dbuf,
     load_sem, halo_send, halo_recv, swap_send, swap_recv,
     ring_send, ring_recv, sib_send, sib_recv,
-    a_send, a_recv, a_self, d_send, d_recv, d_self,
+    a_send, a_recv, a_self, d_send, d_recv, d_self, plane_sem,
 ):
     tm = lax.axis_index("tm")
     sp = lax.axis_index("space")
@@ -68,92 +68,73 @@
     sibling = (col * 2 + 1 - c, sp)
     z_ids = ((tm, h * ZS + zp), (tm, h * ZS + zm))
     stays = c == h
-    block = c * ZS + z
-    last = YH * ZS - 1
+    away = jnp.logical_not(stays)
+    work = (col * 2 + h, c * ZS + z)
 
     loads = []
     for i, (src, dst) in enumerate(
         [
-            (gain_conv, gc), (conv_w.at[1], cw.at[1]), (conv_w.at[0], cw.at[0]),
+            (video, vid), (gain_conv, gc), (conv_w.at[1], cw.at[1]), (conv_w.at[0], cw.at[0]),
             (conv_w.at[2], cw.at[2]), (gain_space, gs), (wq, wq_v), (wk, wk_v), (wv, wv_v), (wo, wo_v),
             (gain_time, gt), (tq, tq_v), (tk, tk_v), (tv, tv_v), (to, to_v),
         ]
     ):
         loads.append(pltpu.make_async_copy(src, dst, load_sem.at[i]))
-        loads[-1].start()
-
-    own_load = pltpu.make_async_copy(video, vid, load_sem.at[14])
-
-    @pl.when(stays)
-    def _():
-        own_load.start()
+    for load in loads[:6]:
+        load.start()
 
     barrier = pltpu.get_barrier_semaphore()
 
     def greet(i, carry):
-        other_tm = i // 2
-        other_sp = lax.rem(i, 2) * ZS + z
-
-        @pl.when(jnp.logical_or(other_tm != tm, other_sp != sp))
-        def _():
-            pl.semaphore_signal(barrier, inc=1, device_id=(other_tm, other_sp), device_id_type=MESH)
-
-        return carry
-
-    lax.fori_loop(0, TM * YH, greet, 0)
-
-    def greet_z(i, carry):
+        other_c, other_h = lax.rem(i, 2), i // 2
+
+        @pl.when(jnp.logical_or(other_c != c, other_h != h))
+        def _():
+            other = (col * 2 + other_c, other_h * ZS + z)
+            pl.semaphore_signal(barrier, inc=1, device_id=other, device_id_type=MESH)
+
         for other_z in (zp, zm):
-            other = (col * 2 + lax.rem(i, 2), (i // 2) * ZS + other_z)
+            other = (col * 2 + other_c, other_h * ZS + other_z)
             pl.semaphore_signal(barrier, inc=1, device_id=other, device_id_type=MESH)
         return carry
 
-    lax.fori_loop(0, CORES * YH, greet_z, 0)
-    pl.semaphore_wait(barrier, TM * YH - 1 + 2 * CORES * YH)
-
-    def place(s):
-        return (col * 2 + lax.div(s, ZS), c * ZS + lax.rem(s, ZS))
-
-    sends_down = sp < last
-    sends_up = sp > 0
-    gets_down = block > 0
-    gets_up = block < last
+    lax.fori_loop(0, CORES * YH, greet, 0)
+    flips = [(tm + 2 * bit - 4 * bit * lax.rem(col // bit, 2), sp) for bit in (1, 2, 4)]
+    for flip in flips:
+        pl.semaphore_signal(barrier, inc=1, device_id=flip, device_id_type=MESH)
+    pl.semaphore_wait(barrier, 3 * CORES * YH - 1 + len(flips))
+
+    def hear(k):
+        if k:
+            pl.semaphore_wait(plane_sem.at[k - 1], 1)
+        if k < len(flips):
+            pl.semaphore_signal(plane_sem.at[k], inc=1, device_id=flips[k], device_id_type=MESH)
+
+    hear(0)
+
+    has_up = sp > 0
+    has_down = sp < YH * ZS - 1
     to_down = pltpu.make_async_remote_copy(
         src_ref=video.at[pl.ds(W, W)], dst_ref=halo.at[0], send_sem=halo_send.at[0], recv_sem=halo_recv.at[0],
-        device_id=place(jnp.minimum(sp + 1, last)), device_id_type=MESH,
+        device_id=(tm, jnp.minimum(sp + 1, YH * ZS - 1)), device_id_type=MESH,
     )
     to_up = pltpu.make_async_remote_copy(
         src_ref=video.at[pl.ds(0, W)], dst_ref=halo.at[1], send_sem=halo_send.at[1], recv_sem=halo_recv.at[1],
-        device_id=place(jnp.maximum(sp - 1, 0)), device_id_type=MESH,
-    )
-    swap = pltpu.make_async_remote_copy(
-        src_ref=video, dst_ref=vid, send_sem=swap_send, recv_sem=swap_recv,
-        device_id=place(sp), device_id_type=MESH,
-    )
-
-    away = jnp.logical_not(stays)
-
-    @pl.when(away)
-    def _():
-        swap.start()
-
-    @pl.when(sends_down)
+        device_id=(tm, jnp.maximum(sp - 1, 0)), device_id_type=MESH,
+    )
+
+    @pl.when(has_down)
     def _():
         to_down.start()
 
-    @pl.when(sends_up)
+    @pl.when(has_up)
     def _():
         to_up.start()
 
-    @pl.when(stays)
-    def _():
-        own_load.wait()
-
-    @pl.when(away)
-    def _():
-        swap.wait_recv()
-
+    for load in loads[6:]:
+        load.start()
     loads[0].wait()
+    loads[1].wait()
     col_index = lax.broadcasted_iota(jnp.int32, (W, D), 0)
 
     def activate(row, raw):
@@ -167,11 +148,11 @@
 
     activate(1, vid[0:W])
     activate(2, vid[W:T])
-    loads[1].wait()
+    loads[2].wait()
     conv_acc[...] = vid[...].astype(F32) + dot(act3[W : 3 * W], cw[1])
-    loads[2].wait()
+    loads[3].wait()
     conv_acc[W:T] += dot(act3[W : 2 * W], cw[0])
-    loads[3].wait()
+    loads[4].wait()
     conv_acc[0:W] += dot(act3[2 * W : 3 * W], cw[2])
 
     my_ring = jnp.where(stays, 0, 1)
@@ -194,6 +175,17 @@
             device_id=z_ids[side], device_id_type=MESH,
         )
 
+    def swap_piece(part):
+        return pltpu.make_async_remote_copy(
+            src_ref=n_out.at[pl.ds(part * QUARTER, QUARTER)], dst_ref=rows_of(1, 0, 0, part * QUARTER, QUARTER),
+            send_sem=swap_send.at[part], recv_sem=swap_recv.at[part], device_id=work, device_id_type=MESH,
+        )
+
+    swap_conv = pltpu.make_async_remote_copy(
+        src_ref=ac_mine, dst_ref=ac_t, send_sem=swap_send.at[4], recv_sem=swap_recv.at[4],
+        device_id=work, device_id_type=MESH,
+    )
+
     def sib_piece(ring, side, dist, half):
         ref = rows_of(ring, side, dist, half * HALF, HALF)
         return pltpu.make_async_remote_copy(
@@ -221,27 +213,47 @@
             conv_acc[part] += dot(act3[3 * row * W : (3 * row + 1) * W], cw[tap])
 
         after_conv = conv_acc[part].astype(BF)
-        ac_t[part] = after_conv
-        at = pl.multiple_of(my_ring * T + row * W, PIECE)
-        nall[pl.ds(at, W)] = channel_norm(after_conv.astype(F32), gs[...]).astype(BF)
-        for quarter in (2 * row, 2 * row + 1):
-            for side in range(2):
-                ring_piece(side, 0, quarter).start()
-        sib_piece(my_ring, 0, 0, row).start()
-
-    loads[4].wait()
-    finish_row(0, gets_down, to_down, 0)
-    finish_row(1, gets_up, to_up, 2)
+        normed = channel_norm(after_conv.astype(F32), gs[...]).astype(BF)
+
+        @pl.when(stays)
+        def _():
+            ac_t[part] = after_conv
+            nall[part] = normed
+            for quarter in (2 * row, 2 * row + 1):
+                for side in range(2):
+                    ring_piece(side, 0, quarter).start()
+            sib_piece(0, 0, 0, row).start()
+
+        @pl.when(away)
+        def _():
+            ac_mine[part] = after_conv
+            n_out[part] = normed
+            for quarter in (2 * row, 2 * row + 1):
+                swap_piece(quarter).start()
 
     loads[5].wait()
-    query = dot(nall[pl.ds(pl.multiple_of(my_ring * T, T), T)], wq_v[...]).astype(BF)
-    loads[6].wait()
-    q_v[...] = (dot_t(query, wk_v[...]) * (SCALE * LOG2E)).astype(BF)
-    for i in range(7, 14):
+    finish_row(0, has_up, to_down, 0)
+    finish_row(1, has_down, to_up, 2)
+
+    hear(1)
+
+    for i in range(6, 15):
         loads[i].wait()
     wvo[...] = dot(wv_v[...], wo_v[...]).astype(BF)
     tw[:, 0:D] = (dot_t(tq_v[...], tk_v[...]) * (SCALE * LOG2E)).astype(BF)
     tw[:, D : 2 * D] = dot(tv_v[...], to_v[...]).astype(BF)
+
+    @pl.when(away)
+    def _():
+        for part in range(4):
+            swap_piece(part).wait_recv()
+            for side in range(2):
+                ring_piece(side, 0, part).start()
+            if part % 2 == 1:
+                sib_piece(1, 0, 0, part // 2).start()
+
+    query = dot(nall[pl.ds(pl.multiple_of(my_ring * T, T), T)], wq_v[...]).astype(BF)
+    q_v[...] = (dot_t(query, wk_v[...]) * (SCALE * LOG2E)).astype(BF)
     m_v[...] = jnp.full(m_v.shape, -1e30, F32)
     l_v[...] = jnp.zeros(l_v.shape, F32)
     acc_v[...] = jnp.zeros(acc_v.shape, F32)
@@ -278,7 +290,7 @@
     before_1 = (
         lambda: other(0),
         lambda: other(1),
-        lambda: (own(1, 0), own(1, 1)),
+        lambda: (own(1, 0), own(1, 1), swap_conv.start()),
         lambda: (own(2, 0), other(2)),
         lambda: own(2, 1),
         lambda: (own(3, 0), other(3)),
@@ -314,7 +326,9 @@
         m_v[rows] = jnp.broadcast_to(m_new, (l_new.shape[0], 128))
         acc_v[rows] = acc_v[rows] * alpha + dot(p.astype(BF), keys)
 
+    hear(2)
     lax.fori_loop(0, STEPS - 1, attend, 0)
+    hear(3)
 
     frame = col * 2 + h
     home = c * ZS + z
@@ -352,12 +366,16 @@
 
     arrive(STEPS - 1)
 
-    for half in range(2):
-        part = slice(half * HALF, (half + 1) * HALF)
+    @pl.when(away)
+    def _():
+        swap_conv.wait_recv()
+
+    for start, stop in ((0, 6), (6, PIECES)):
+        part = slice(start * PIECE, stop * PIECE)
         attend_rows(part, nall[(STEPS - 1) * KEYS :])
         mixed = (acc_v[part] / l_v[part, 0:1]).astype(BF)
         as_t[part] = (ac_t[part].astype(F32) + dot(mixed, wvo[...])).astype(BF)
-        lax.fori_loop(half * (PIECES // 2), (half + 1) * (PIECES // 2), a_start, 0)
+        lax.fori_loop(start, stop, a_start, 0)
 
     first = lax.rem(13 * tm, TM)
     has_second = first < PIECES - TM
@@ -396,15 +414,6 @@
 
             return carry
 
-        lax.fori_loop(0, FRAMES, wait_piece, 0)
-        x = tbuf[slot]
-        normed = channel_norm(x.astype(F32), gt[...]).astype(BF)
-        qv = dot(normed, tw[...]).astype(BF)
-        s = jnp.where(allowed, dot_t(qv[:, 0:D], normed), -1e30)
-        p = jnp.exp2(s - jnp.max(s, axis=1, keepdims=True))
-        total = jnp.sum(p, axis=1, keepdims=True)
-        dbuf[slot] = (x.astype(F32) + dot(p.astype(BF), qv[:, D:]) / total).astype(BF)
-
         def d_start(f, carry):
             @pl.when(f == tm)
             def _():
@@ -416,7 +425,19 @@
 
             return carry
 
-        lax.fori_loop(0, FRAMES, d_start, 0)
+        middle = rows // 2
+        for begin, end in ((0, middle), (middle, rows)):
+            lax.fori_loop(begin // PIECE, end // PIECE, wait_piece, 0)
+            x = tbuf[slot, begin:end]
+            normed = channel_norm(x.astype(F32), gt[...]).astype(BF)
+            qv = dot(normed, tw[...]).astype(BF)
+            tn[begin:end] = normed
+            tv_n[begin:end] = qv[:, D:]
+            s = jnp.where(allowed[begin:end, 0:end], dot_t(qv[:, 0:D], tn[0:end]), -1e30)
+            p = jnp.exp2(s - jnp.max(s, axis=1, keepdims=True))
+            total = jnp.sum(p, axis=1, keepdims=True)
+            dbuf[slot, begin:end] = (x.astype(F32) + dot(p.astype(BF), tv_n[0:end]) / total).astype(BF)
+            lax.fori_loop(begin // PIECE, end // PIECE, d_start, 0)
 
     temporal(0, first)
 
@@ -461,17 +482,19 @@
 
     lax.fori_loop(0, FRAMES, d_sent, 0)
 
-    @pl.when(sends_down)
+    @pl.when(has_down)
     def _():
         to_down.wait_send()
 
-    @pl.when(sends_up)
+    @pl.when(has_up)
     def _():
         to_up.wait_send()
 
     @pl.when(away)
     def _():
-        swap.wait_send()
+        swap_conv.wait_send()
+        for part in range(4):
+            swap_piece(part).wait_send()
 
     for dist in range(ZS // 2 + 1):
         for side in range(2):
@@ -495,13 +518,13 @@
         out_specs=pl.BlockSpec(memory_space=pl.ANY),
         scratch_shapes=[
             vm((T, D), BF), vm((2, W, D), BF), vm((1, D), F32), vm((1, D), F32), vm((1, D), F32),
-            vm((3, 3 * D, D), BF), *[vm((D, D), BF) for _ in range(9)], vm((D, 2 * D), BF),
-            vm((4 * W, 3 * D), BF), vm((T, D), F32), vm((T, D), BF), vm((2 * ZS * T, D), BF),
+            vm((3, 3 * D, D), BF), *[vm((D, D), BF) for _ in range(9)], vm((D, 2 * D), BF), vm((FRAMES * PIECE, D), BF), vm((FRAMES * PIECE, D), BF),
+            vm((4 * W, 3 * D), BF), vm((T, D), F32), vm((T, D), BF), vm((T, D), BF), vm((T, D), BF), vm((2 * ZS * T, D), BF),
             vm((T, D), BF), vm((T, 128), F32), vm((T, 128), F32), vm((T, D), F32), vm((T, D), BF),
             vm((2, FRAMES * PIECE, D), BF), vm((2, FRAMES * PIECE, D), BF),
-            dma((15,)), dma((2,)), dma((2,)), dma, dma,
+            dma((15,)), dma((2,)), dma((2,)), dma((5,)), dma((5,)),
             dma((2, 4, 4)), dma((2, 4, 4)), dma((2, 5, 2)), dma((2, 5, 2)),
-            dma((PIECES,)), dma((2, FRAMES)), dma((2,)), dma((2, FRAMES)), dma((PIECES,)), dma((2,)),
+            dma((PIECES,)), dma((2, FRAMES)), dma((2,)), dma((2, FRAMES)), dma((PIECES,)), dma((2,)), pltpu.SemaphoreType.REGULAR((3,)),
         ],
         compiler_params=pltpu.CompilerParams(
             collective_id=0, has_side_effects=True, vmem_limit_bytes=56 * 1024 * 1024

time: 63.7 us -> 61.8 us (0.970)
  Pallas kernels: 61.9 us -> 59.9 us
    pallas_call x1, Pallas kernels: 61.9 us -> 59.9 us  [local(): pl.pallas_call(kernel, out_shape=jax.ShapeDtypeStruct((T, D), BF), in_spe...]
where the time goes in v4:
time: 61.8 us; the launch traced here: 61.6 us
  Pallas kernels  59.9 us (97%)
  local copies, waits for them, and re-layouts  1.72 us (3%)
    pallas_call x1, Pallas kernels, local(): pl.pallas_call(kernel, out_shape=jax.ShapeDtypeStruct((T, D), BF), in_spe...  59.9 us
    unnamed x1, local copies, waits for them, and re-layouts  1.72 us

profile of v4, /device:TPU:1, one launch (start us, length us, event | category | flops | bytes accessed | tf_op | source)
XLA Modules:
  0.0 61.6 jit_solution(1376215194943406099)
XLA Ops:
  0.0 59.9 %shard_map.127 = bf16[320,512]{1,0:T(8,128)(2,1)} custom-call(bf16[320,512]{1,0:T(8,128)(2,1)} %bitcast.8, f32[1,512]{1,0:T(1,128)} %bitcast.9, bf16[3,1536,512]{2,1,0:T(8,128)(2,1)} %bitcast.6, f32[1,512]{1,0:T(1,128)} %bitcast.10, bf16[512,512]{1,0:T(8,128)(2,1)} %wq.1, bf16[512,512]{1,0:T(8,128)(2,1)} %wk.1, bf16[512,512]{1,0:T(8,128)(2,1)} %wv.1, ...), custom_call_target="tpu_custom_call" | custom-call | tf_op jit(solution)/shard_map/pallas_call | solution.py:514
  59.9 1.7 %copy.15 = bf16[1,2,160,512]{3,2,1,0:T(8,128)(2,1)} copy(bf16[1,2,160,512]{3,2,1,0:T(8,128)(2,1)} %bitcast.7) | data formatting | bytes 655360

commit v5 on v4

--- a/solution.py
+++ b/solution.py
@@ -71,6 +71,19 @@
     away = jnp.logical_not(stays)
     work = (col * 2 + h, c * ZS + z)
 
+    barrier = pltpu.get_barrier_semaphore()
+    flips = [(tm + 2 * bit - 4 * bit * lax.rem(col // bit, 2), sp) for bit in (1, 2, 4)]
+    across = (tm, (1 - h) * ZS + z)
+    near = [*z_ids, sibling, across, (sibling[0], across[1]), *flips]
+    for other in near:
+        pl.semaphore_signal(barrier, inc=1, device_id=other, device_id_type=MESH)
+    crosses = jnp.logical_or(sp == ZS - 1, sp == ZS)
+
+    @pl.when(crosses)
+    def _():
+        other = (tm, 2 * ZS - 1 - sp)
+        pl.semaphore_signal(barrier, inc=1, device_id=other, device_id_type=MESH)
+
     loads = []
     for i, (src, dst) in enumerate(
         [
@@ -83,26 +96,7 @@
     for load in loads[:6]:
         load.start()
 
-    barrier = pltpu.get_barrier_semaphore()
-
-    def greet(i, carry):
-        other_c, other_h = lax.rem(i, 2), i // 2
-
-        @pl.when(jnp.logical_or(other_c != c, other_h != h))
-        def _():
-            other = (col * 2 + other_c, other_h * ZS + z)
-            pl.semaphore_signal(barrier, inc=1, device_id=other, device_id_type=MESH)
-
-        for other_z in (zp, zm):
-            other = (col * 2 + other_c, other_h * ZS + other_z)
-            pl.semaphore_signal(barrier, inc=1, device_id=other, device_id_type=MESH)
-        return carry
-
-    lax.fori_loop(0, CORES * YH, greet, 0)
-    flips = [(tm + 2 * bit - 4 * bit * lax.rem(col // bit, 2), sp) for bit in (1, 2, 4)]
-    for flip in flips:
-        pl.semaphore_signal(barrier, inc=1, device_id=flip, device_id_type=MESH)
-    pl.semaphore_wait(barrier, 3 * CORES * YH - 1 + len(flips))
+    pl.semaphore_wait(barrier, len(near) + jnp.where(crosses, 1, 0))
 
     def hear(k):
         if k:

time: 61.8 us -> 61.6 us (level)
  no operation moved by 1% of the time
where the time goes in v5:
time: 61.6 us; the launch traced here: 61.4 us
  Pallas kernels  59.7 us (97%)
  local copies, waits for them, and re-layouts  1.72 us (3%)
    pallas_call x1, Pallas kernels, local(): pl.pallas_call(kernel, out_shape=jax.ShapeDtypeStruct((T, D), BF), in_spe...  59.7 us
    unnamed x1, local copies, waits for them, and re-layouts  1.72 us

profile of v5, /device:TPU:1, one launch (start us, length us, event | category | flops | bytes accessed | tf_op | source)
XLA Modules:
  0.0 61.4 jit_solution(4876382771868418049)
XLA Ops:
  0.0 59.7 %shard_map.127 = bf16[320,512]{1,0:T(8,128)(2,1)} custom-call(bf16[320,512]{1,0:T(8,128)(2,1)} %bitcast.8, f32[1,512]{1,0:T(1,128)} %bitcast.9, bf16[3,1536,512]{2,1,0:T(8,128)(2,1)} %bitcast.6, f32[1,512]{1,0:T(1,128)} %bitcast.10, bf16[512,512]{1,0:T(8,128)(2,1)} %wq.1, bf16[512,512]{1,0:T(8,128)(2,1)} %wk.1, bf16[512,512]{1,0:T(8,128)(2,1)} %wv.1, ...), custom_call_target="tpu_custom_call" | custom-call | tf_op jit(solution)/shard_map/pallas_call | solution.py:508
  59.7 1.7 %copy.15 = bf16[1,2,160,512]{3,2,1,0:T(8,128)(2,1)} copy(bf16[1,2,160,512]{3,2,1,0:T(8,128)(2,1)} %bitcast.7) | data formatting | bytes 655360

commit v6 on v5

--- a/solution.py
+++ b/solution.py
@@ -369,7 +369,7 @@
         attend_rows(part, nall[(STEPS - 1) * KEYS :])
         mixed = (acc_v[part] / l_v[part, 0:1]).astype(BF)
         as_t[part] = (ac_t[part].astype(F32) + dot(mixed, wvo[...])).astype(BF)
-        lax.fori_loop(start, stop, a_start, 0)
+        lax.fori_loop(start, stop, a_start, 0, unroll=True)
 
     first = lax.rem(13 * tm, TM)
     has_second = first < PIECES - TM
@@ -431,7 +431,7 @@
             p = jnp.exp2(s - jnp.max(s, axis=1, keepdims=True))
             total = jnp.sum(p, axis=1, keepdims=True)
             dbuf[slot, begin:end] = (x.astype(F32) + dot(p.astype(BF), tv_n[0:end]) / total).astype(BF)
-            lax.fori_loop(begin // PIECE, end // PIECE, d_start, 0)
+            lax.fori_loop(begin // PIECE, end // PIECE, d_start, 0, unroll=True)
 
     temporal(0, first)
 

time: 61.6 us -> 61.9 us (level)
  no operation moved by 1% of the time
where the time goes in v6:
time: 61.9 us; the launch traced here: 61.8 us
  Pallas kernels  60 us (97%)
  local copies, waits for them, and re-layouts  1.72 us (3%)
    pallas_call x1, Pallas kernels, local(): pl.pallas_call(kernel, out_shape=jax.ShapeDtypeStruct((T, D), BF), in_spe...  60 us
    unnamed x1, local copies, waits for them, and re-layouts  1.72 us

profile of v6, /device:TPU:1, one launch (start us, length us, event | category | flops | bytes accessed | tf_op | source)
XLA Modules:
  0.0 61.8 jit_solution(357949557769133789)
XLA Ops:
  0.0 60.0 %shard_map.127 = bf16[320,512]{1,0:T(8,128)(2,1)} custom-call(bf16[320,512]{1,0:T(8,128)(2,1)} %bitcast.8, f32[1,512]{1,0:T(1,128)} %bitcast.9, bf16[3,1536,512]{2,1,0:T(8,128)(2,1)} %bitcast.6, f32[1,512]{1,0:T(1,128)} %bitcast.10, bf16[512,512]{1,0:T(8,128)(2,1)} %wq.1, bf16[512,512]{1,0:T(8,128)(2,1)} %wk.1, bf16[512,512]{1,0:T(8,128)(2,1)} %wv.1, ...), custom_call_target="tpu_custom_call" | custom-call | tf_op jit(solution)/shard_map/pallas_call | solution.py:508
  60.0 1.7 %copy.15 = bf16[1,2,160,512]{3,2,1,0:T(8,128)(2,1)} copy(bf16[1,2,160,512]{3,2,1,0:T(8,128)(2,1)} %bitcast.7) | data formatting | bytes 655360
